TPU v7x, 256 devices: a whole 4x4x8 slice. The times are simulated.
256 devices in a mesh: mesh: 16 (over x_hi, y, core), four: 16 (over x_lo, z).
Axes of the slice: x: 4 (x_hi: 2, x_lo: 2; x = x_hi * 2 + x_lo), y: 4, z: 8, core: 2. Of those that a mesh axis runs over, the one named last changes fastest.
Arguments:
- adj_modes: float32 [3, 256, 64, 4096], P(None, 'four', None, 'mesh'), may hold values from -1 to 1
- base_flow: bfloat16 [12, 256, 64, 4096], P(None, None, 'four', 'mesh'), may hold values from -6 to 6
- geometry: float32 [4, 64, 4096], P(None, None, 'mesh'), may hold values from -1 to 1
- mass: float32 [64, 4096], P(None, 'mesh'), may hold values from 0.2 to 2
- connect: int32 [64, 4096], P(None, 'mesh'), may hold values from 0 to 12824, as said below
- edge_nodes: int32 [16, 2, 225], P('mesh'), may hold values from 0 to 12824, as said below
Outputs:
- adj_next: float32 [3, 256, 64, 4096], P(None, 'four', None, 'mesh')
Inputs may be any that keep to these rules, and one draw needn't show every extreme that they name: `connect`: columns p * 256 to (p + 1) * 256 - 1 form partition p. Each partition numbers its 12825 nodes from 0; element nodes at the same place share an id, and every id is used. edge_nodes[p, 1] lists the ids of partition p's nodes that coincide with nodes of partition p + 1 (mod 16), in the same order in which edge_nodes[p + 1, 0] lists them; the two lists of a partition are disjoint, and no other node is shared between partitions.
All inputs are finite; a program needn't handle non-finite values.
Results may differ from a plain program's by a relative error of at most 0.0003.
Values sent between devices are 32-bit elements; how exact they have to be, the bound alone decides.
A program may use at most 128 MiB of HBM per device.

v0:
```python
import math

import jax
import jax.numpy as jnp
from jax import lax
from jax.sharding import PartitionSpec as P

NP = 8
PLANES = 256
UNIQUE = 12825


STEP_SIZE = 0.1
HIGH = lax.Precision.HIGHEST


def padded(shard, sides, width):
    for axis, dim in sides:
        count, length = (lax.axis_size(axis), shard.shape[dim])
        up = [(i, (i + 1) % count) for i in range(count)]
        down = [(j, i) for i, j in up]
        last = lax.slice_in_dim(shard, length - width, length, axis=dim)
        leading = lax.slice_in_dim(shard, 0, width, axis=dim)
        before = lax.ppermute(last, axis, up)
        after = lax.ppermute(leading, axis, down)
        shard = jnp.concatenate([before, shard, after], axis=dim)
    return shard


def legendre_values(degree, point):
    before = 1.0
    current = point
    for order in range(1, degree):
        after = ((2 * order + 1) * point * current - order * before) / (order + 1)
        before = current
        current = after
    return (current, before)


def gll_derivative(points_n):
    degree = points_n - 1
    points = []
    for index in range(points_n):
        point = -math.cos(math.pi * index / degree)
        for sweep in range(100):
            top_val, below_val = legendre_values(degree, point)
            point = point - (point * top_val - below_val) / (points_n * top_val)
        points.append(point)
    values = [legendre_values(degree, point)[0] for point in points]
    deriv_rows = []
    for row_index in range(points_n):
        row_vals = []
        for col_index in range(points_n):
            if row_index != col_index:
                row_vals.append(
                    values[row_index]
                    / (values[col_index] * (points[row_index] - points[col_index]))
                )
            else:
                row_vals.append(0.0)
        deriv_rows.append(row_vals)
    deriv_rows[0][0] = -degree * (degree + 1) / 4.0
    deriv_rows[degree][degree] = degree * (degree + 1) / 4.0
    deriv_table = jnp.asarray(deriv_rows, jnp.float32)
    identity = jnp.eye(points_n, dtype=jnp.float32)
    return (jnp.kron(deriv_table, identity), jnp.kron(identity, deriv_table))


def plane_tables(planes):
    plane_idx = jnp.arange(planes, dtype=jnp.int32)
    wave_idx = plane_idx // 2
    phase = (plane_idx[:, None] * wave_idx[None, :] % planes).astype(jnp.float32) * (
        2.0 * math.pi / planes
    )
    is_sine = plane_idx % 2 == 1
    synth = jnp.where(is_sine[None, :], jnp.sin(phase), jnp.cos(phase))
    alternate = (1 - 2 * (plane_idx % 2)).astype(jnp.float32)
    synth = synth.at[:, 1].set(alternate)
    scales = jnp.where(wave_idx == 0, 1.0 / planes, 2.0 / planes).astype(jnp.float32)
    analysis = synth.T * scales[:, None]
    return (synth, analysis)


def axial(coef, wave):
    pairs = coef.reshape(coef.shape[0], coef.shape[1] // 2, 2, coef.shape[2], coef.shape[3])
    factor = wave[None, :, None, None]
    return jnp.stack([factor * pairs[:, :, 1], -factor * pairs[:, :, 0]], axis=2).reshape(
        coef.shape
    )


def gradients(coef, geometry, deriv_r, deriv_s):
    along_r = jnp.einsum("mn,fpne->fpme", deriv_r, coef, precision=HIGH)
    along_s = jnp.einsum("mn,fpne->fpme", deriv_s, coef, precision=HIGH)
    grad_x = geometry[0] * along_r + geometry[1] * along_s
    grad_y = geometry[2] * along_r + geometry[3] * along_s
    return (grad_x, grad_y)


def advect(physical, base):
    pieces = []
    for component in range(3):
        total = jnp.zeros(physical.shape[1:], jnp.float32)
        for direction in range(3):
            total = (
                total
                - base[direction].astype(jnp.float32) * physical[3 + 3 * direction + component]
                + physical[direction] * base[3 + 3 * component + direction].astype(jnp.float32)
            )
        pieces.append(total)
    return jnp.stack(pieces)


def assemble(weighted, mass, connect, edges):
    fields_n, planes_dev, points_n, elems_n = weighted.shape
    node_ids = connect.reshape(-1)
    rows = jnp.concatenate([weighted.reshape(fields_n * planes_dev, -1), mass.reshape(1, -1)])
    summed = jnp.zeros((rows.shape[0], UNIQUE), jnp.float32).at[:, node_ids].add(rows)
    lower = edges[0]
    upper = edges[1]
    rims = jnp.stack([summed[:, lower], summed[:, upper]])
    widened = padded(rims, (("mesh", 0),), 1)
    summed = summed.at[:, lower].set(widened[1] + widened[0])
    summed = summed.at[:, upper].set(widened[2] + widened[3])
    spread_back = summed[:, node_ids]
    result = spread_back[:-1] / spread_back[-1:]
    return result.reshape(weighted.shape)


def body(adj_modes, base_flow, geometry, mass, connect, edge_nodes):
    deriv_r, deriv_s = gll_derivative(NP)
    synth, analysis = plane_tables(PLANES)
    planes_dev = adj_modes.shape[1]
    grad_x, grad_y = gradients(adj_modes, geometry, deriv_r, deriv_s)
    pair_first = lax.axis_index("four") * (planes_dev // 2)
    wave = (pair_first + jnp.arange(planes_dev // 2, dtype=jnp.int32)).astype(jnp.float32) * (
        2.0 / PLANES
    )
    grad_z = axial(adj_modes, wave)
    packed = jnp.concatenate([adj_modes, grad_x, grad_y, grad_z])
    spread = lax.all_to_all(packed, "four", split_axis=2, concat_axis=1, tiled=True)
    physical = jnp.einsum("jm,fmne->fjne", synth, spread, precision=HIGH)
    forcing = advect(physical, base_flow)
    forcing_modes = jnp.einsum("mj,fjne->fmne", analysis, forcing, precision=HIGH)
    returned = lax.all_to_all(forcing_modes, "four", split_axis=1, concat_axis=2, tiled=True)
    weighted = mass * (adj_modes + STEP_SIZE * returned)
    return assemble(weighted, mass, connect, edge_nodes[0])


def solution(mesh):
    return jax.shard_map(
        body,
        mesh=mesh,
        in_specs=(
            P(None, "four", None, "mesh"),
            P(None, None, "four", "mesh"),
            P(None, None, "mesh"),
            P(None, "mesh"),
            P(None, "mesh"),
            P("mesh", None, None),
        ),
        out_specs=P(None, "four", None, "mesh"),
        check_vma=False,
    )
```

profile of v0, /device:TPU:2, one launch (start us, length us, event | category | flops | bytes accessed | tf_op | source)
XLA Modules:
  0.0 663.0 jit_solution(6282347393515144535)
XLA Ops:
  2.1 4.8 fusion.53
  7.6 3.7 add_bitcast_fusion.1
  11.3 5.3 pad_maximum_fusion
  16.6 16.3 %copy.127 = f32[12,16,64,256]{3,1,0,2:T(8,128)} copy(f32[12,16,64,256]{3,2,1,0:T(8,128)} %pad_maximum_fusion) | data formatting | bytes 25165824 | tf_op jit(solution)/shard_map/concatenate | solution.py:140
  32.9 10.2 %all-to-all-start = ((f32[12,16,64,256]{3,1,0,2:T(8,128)}), f32[12,16,64,256]{3,1,0,2:T(8,128)}, u32[]{:S(2)}, u32[]{:S(2)}) async-start(f32[12,16,64,256]{3,1,0,2:T(8,128)} %copy.127), calls=%async_computation | async-start | bytes 25165824 | tf_op jit(solution)/shard_map/all_to_all | solution.py:141
  43.2 5.3 fusion.62
  48.5 2.2 copy.155
  50.6 2.1 copy.157
  52.8 2.1 copy.159
  57.0 2.1 copy.158
  63.3 2.1 copy.162
  65.5 2.1 copy.163
  69.7 2.1 copy.165
  76.9 244.7 %all-to-all-done = f32[12,16,64,256]{3,1,0,2:T(8,128)} async-done(((f32[12,16,64,256]{3,1,0,2:T(8,128)}), f32[12,16,64,256]{3,1,0,2:T(8,128)}, u32[]{:S(2)}, u32[]{:S(2)}) %all-to-all-start) | async-done | bytes 12582944 | tf_op jit(solution)/shard_map/all_to_all | solution.py:141
  321.6 11.3 %copy.129 = f32[12,16,16,4,256]{4,2,1,3,0:T(8,128)} copy(f32[12,16,16,4,256]{4,2,0,3,1:T(8,128)} %bitcast.13) | data formatting | bytes 25165824 | tf_op jit(solution)/shard_map/all_to_all | solution.py:141
  333.0 24.3 %convolution_bitcast_fusion = f32[12,256,4,256]{1,3,2,0:T(8,128)S(1)} fusion(f32[12,256,4,256]{3,1,2,0:T(8,128)} %bitcast.106, f32[256,256]{1,0:T(8,128)S(1)} %scatter.19), kind=kOutput, calls=%fused_computation.7 | convolution fusion | flops 9663676416 | bytes 25427968 | tf_op jit(solution)/shard_map/jm,fmne->fjne/dot_general | solution.py:142
  360.7 4.3 fusion.9
  365.0 5.2 copy.142
  370.2 17.1 %all-to-all-start.1 = ((f32[3,256,4,256]{3,2,0,1:T(4,128)}), f32[3,256,4,256]{3,2,0,1:T(4,128)}, u32[]{:S(2)}, u32[]{:S(2)}) async-start(f32[3,256,4,256]{3,2,0,1:T(4,128)} %copy.142), calls=%async_computation.1 | async-start | bytes 6291456 | tf_op jit(solution)/shard_map/all_to_all | solution.py:145
  387.6 70.4 %all-to-all-done.1 = f32[3,256,4,256]{3,2,0,1:T(4,128)} async-done(((f32[3,256,4,256]{3,2,0,1:T(4,128)}), f32[3,256,4,256]{3,2,0,1:T(4,128)}, u32[]{:S(2)}, u32[]{:S(2)}) %all-to-all-start.1) | async-done | bytes 3145760 | tf_op jit(solution)/shard_map/all_to_all | solution.py:145
  458.0 2.6 copy_multiply_fusion
  468.7 6.8 %copy.147 = f32[16384,49]{1,0:T(8,128)} copy(f32[16384,49]{0,1:T(8,128)} %maximum_bitcast_fusion) | data formatting | bytes 6422528 | tf_op jit(solution)/shard_map/concatenate | solution.py:117
  475.5 90.8 %scatter_custom_fusion = f32[49,12825]{0,1:T(8,128)} fusion(s32[16384]{0:T(1024)S(1)} %bitcast.118, f32[16384,49]{1,0:T(8,128)} %copy.147, f32[]{:T(128)} %constant.91.clone.1), kind=kCustom, calls=%fused_computation.9 | custom fusion | flops 802816 | bytes 2514212 | tf_op jit(solution)/shard_map/scatter-add | solution.py:118
  566.3 3.6 gather_fusion.1
  569.9 3.6 gather_fusion
  573.5 5.7 collective-permute-start.1
  579.2 6.7 %scatter_custom_fusion.1 = f32[49,12825]{0,1:T(8,128)} fusion(f32[49,12825]{0,1:T(8,128)} %scatter_custom_fusion, s32[225]{0:T(256)S(1)} %bitcast.127, f32[1,49,225]{1,2,0:T(8,128)S(1)} %collective-permute-done, f32[225,49]{1,0:T(8,128)S(1)} %gather_fusion), kind=kCustom, calls=%fused_computation.83 | custom fusion | flops 11025 | bytes 2751268 | tf_op jit(solution)/shard_map/scatter | solution.py:123
  585.9 6.7 %scatter_custom_fusion.2 = f32[49,12825]{0,1:T(8,128)} fusion(f32[49,12825]{0,1:T(8,128)} %scatter_custom_fusion.1, s32[225]{0:T(256)S(1)} %bitcast.125, f32[1,49,225]{1,2,0:T(8,128)S(1)} %collective-permute-done.1, f32[225,49]{1,0:T(8,128)S(1)} %gather_fusion.1), kind=kCustom, calls=%fused_computation.80 | custom fusion | flops 11025 | bytes 2751268 | tf_op jit(solution)/shard_map/scatter | solution.py:124
  592.6 57.3 %gather_fusion.2 = f32[16384,49]{1,0:T(8,128)} fusion(f32[49,12825]{0,1:T(8,128)} %scatter_custom_fusion.2, s32[16384]{0:T(1024)S(1)} %broadcast_clamp_fusion), kind=kCustom, calls=%fused_computation.2 | custom fusion | bytes 6488064 | tf_op jit(solution)/shard_map/gather | solution.py:125
  649.8 6.8 %copy.148 = f32[16384,49]{0,1:T(8,128)} copy(f32[16384,49]{1,0:T(8,128)} %gather_fusion.2) | data formatting | bytes 6422528 | tf_op jit(solution)/shard_map/gather | solution.py:125
  657.7 2.1 slice_divide_fusion
  659.8 2.6 copy.170
  (71 shorter events, 29.0 us)
Async XLA Ops:
  2.1 4.8 copy-start
  32.9 288.7 %all-to-all-start = ((f32[12,16,64,256]{3,1,0,2:T(8,128)}), f32[12,16,64,256]{3,1,0,2:T(8,128)}, u32[]{:S(2)}, u32[]{:S(2)}) async-start(f32[12,16,64,256]{3,1,0,2:T(8,128)} %copy.127), calls=%async_computation | async-start | bytes 25165824 | tf_op jit(solution)/shard_map/all_to_all | solution.py:141
  332.9 24.3 %copy-start.1 = (bf16[1,256,4,256]{1,3,2,0:T(8,128)(2,1)S(1)}, bf16[1,256,4,256]{1,3,2,0:T(8,128)(2,1)}, u32[]{:S(2)}) copy-start(bf16[1,256,4,256]{1,3,2,0:T(8,128)(2,1)} %copy.155) | copy-start | bytes 1572868
  332.9 24.3 %copy-start.2 = (bf16[1,256,4,256]{1,3,2,0:T(8,128)(2,1)S(1)}, bf16[1,256,4,256]{1,3,2,0:T(8,128)(2,1)}, u32[]{:S(2)}) copy-start(bf16[1,256,4,256]{1,3,2,0:T(8,128)(2,1)} %copy.157) | copy-start | bytes 1572868
  332.9 24.3 %copy-start.3 = (bf16[1,256,4,256]{1,3,2,0:T(8,128)(2,1)S(1)}, bf16[1,256,4,256]{1,3,2,0:T(8,128)(2,1)}, u32[]{:S(2)}) copy-start(bf16[1,256,4,256]{1,3,2,0:T(8,128)(2,1)} %copy.159) | copy-start | bytes 1572868
  333.0 24.3 %copy-start.4 = (bf16[1,256,4,256]{1,3,2,0:T(8,128)(2,1)S(1)}, bf16[1,256,4,256]{1,3,2,0:T(8,128)(2,1)}, u32[]{:S(2)}) copy-start(bf16[1,256,4,256]{1,3,2,0:T(8,128)(2,1)} %copy.156) | copy-start | bytes 1572868
  333.0 24.3 %copy-start.5 = (bf16[1,256,4,256]{1,3,2,0:T(8,128)(2,1)S(1)}, bf16[1,256,4,256]{1,3,2,0:T(8,128)(2,1)}, u32[]{:S(2)}) copy-start(bf16[1,256,4,256]{1,3,2,0:T(8,128)(2,1)} %copy.158) | copy-start | bytes 1572868
  333.0 24.3 %copy-start.7 = (bf16[1,256,4,256]{1,3,2,0:T(8,128)(2,1)S(1)}, bf16[1,256,4,256]{1,3,2,0:T(8,128)(2,1)}, u32[]{:S(2)}) copy-start(bf16[1,256,4,256]{1,3,2,0:T(8,128)(2,1)} %copy.160) | copy-start | bytes 1572868
  357.3 1.0 copy-start.8
  357.3 1.2 copy-start.10
  357.3 1.3 copy-start.11
  358.7 1.0 copy-start.6
  358.7 1.2 copy-start.9
  358.7 1.4 copy-start.12
  370.2 17.2 %copy-start.13 = (f32[64,256]{1,0:T(8,128)S(1)}, f32[64,256]{1,0:T(8,128)}, u32[]{:S(2)}) copy-start(f32[64,256]{1,0:T(8,128)} %param.12) | copy-start | bytes 196612
  370.2 17.2 %copy-start.14 = (s32[64,256]{1,0:T(8,128)S(1)}, s32[64,256]{1,0:T(8,128)}, u32[]{:S(2)}) copy-start(s32[64,256]{1,0:T(8,128)} %param.13) | copy-start | bytes 196612
  370.2 17.3 %copy-start.15 = (s32[1,2,225]{2,1,0:T(2,128)S(1)}, s32[1,2,225]{2,1,0:T(2,128)}, u32[]{:S(2)}) copy-start(s32[1,2,225]{2,1,0:T(2,128)} %param.14) | copy-start | bytes 5404
  370.2 87.8 %all-to-all-start.1 = ((f32[3,256,4,256]{3,2,0,1:T(4,128)}), f32[3,256,4,256]{3,2,0,1:T(4,128)}, u32[]{:S(2)}, u32[]{:S(2)}) async-start(f32[3,256,4,256]{3,2,0,1:T(4,128)} %copy.142), calls=%async_computation.1 | async-start | bytes 6291456 | tf_op jit(solution)/shard_map/all_to_all | solution.py:145
  569.8 9.4 %collective-permute-start = (f32[1,49,225]{1,2,0:T(8,128)S(1)}, f32[1,49,225]{1,2,0:T(8,128)S(1)}, u32[]{:S(2)}, u32[]{:S(2)}) collective-permute-start(f32[1,49,225]{1,2,0:T(8,128)S(1)} %bitcast.121), channel_id=1, source_target_pairs={{0,16},{16,32},{32,48},{48,64},{64,80},{80,96},{96,112},{112,128},... | collective-permute-start | bytes 132308 | tf_op jit(solution)/shard_map/ppermute | solution.py:24
  573.5 12.4 %collective-permute-start.1 = (f32[1,49,225]{1,2,0:T(8,128)S(1)}, f32[1,49,225]{1,2,0:T(8,128)S(1)}, u32[]{:S(2)}, u32[]{:S(2)}) collective-permute-start(f32[1,49,225]{1,2,0:T(8,128)S(1)} %bitcast.122), channel_id=1, source_target_pairs={{16,0},{32,16},{48,32},{64,48},{80,64},{96,80},{112,96},{128,112},... | collective-permute-start | bytes 132308 | tf_op jit(solution)/shard_map/ppermute | solution.py:25
where the time goes:
time: 671 us; the launch traced here: 663 us
  waiting for transfers between devices  315 us (47%)
  local copies, waits for them, and re-layouts  153 us (23%)
  other arithmetic  124 us (18%)
  matrix products  37.1 us (6%)
  starting transfers between devices  33.2 us (5%)
    all_to_all x1, waiting for transfers between devices, body(): lax.all_to_all(packed, 'four', split_axis=2, concat_axis=1, tiled=True)  245 us
    scatter-add x1, other arithmetic, assemble(): jnp.zeros((rows.shape[0], UNIQUE), jnp.float32).at[:, node_ids].add(rows)  90.8 us
    all_to_all x1, waiting for transfers between devices, body(): lax.all_to_all(forcing_modes, 'four', split_axis=1, concat_axis=2, tiled=...  70.4 us
    gather x2, local copies, waits for them, and re-layouts, assemble(): spread_back = summed[:, node_ids]  64 us
    unnamed x48, local copies, waits for them, and re-layouts  31.4 us
    dot_general x1, matrix products, body(): physical = jnp.einsum('jm,fmne->fjne', synth, spread, precision=HIGH)  24.3 us
    all_to_all x1, starting transfers between devices, body(): lax.all_to_all(forcing_modes, 'four', split_axis=1, concat_axis=2, tiled=...  17.1 us
    concatenate x1, local copies, waits for them, and re-layouts, body(): packed = jnp.concatenate([adj_modes, grad_x, grad_y, grad_z])  16.3 us
  transfers between devices with their start and end apart: 4, of which 2 were waited for; matrix products, arithmetic and copies ran while one was open for 7% of the time, Pallas kernels for 0%

commit v1 on v0

v1 whole, which is shorter than its diff:
```python
import functools
import math

import jax
import jax.numpy as jnp
import numpy as np
from jax import lax
from jax.experimental import pallas as pl
from jax.experimental.pallas import tpu as pltpu
from jax.sharding import PartitionSpec as P

NP = 8
NODES = 64
PLANES = 256
UNIQUE = 12825
E_DEV = 256
POINTS = NODES * E_DEV
EXTRA = POINTS - UNIQUE
LIST_ROWS = (EXTRA + 1023) // 1024 * 8
RIM = 225
RIM_PAD = 512
HALVES = 2
LANES = E_DEV // HALVES
GROUP = 16
COEFS = PLANES // GROUP
STEP_SIZE = 0.1
HIGH = lax.Precision.HIGHEST
MESH = pl.DeviceIdType.MESH
VMEM_LIMIT = 60 * 2**20


def legendre_values(degree, point):
    before = 1.0
    current = point
    for order in range(1, degree):
        after = ((2 * order + 1) * point * current - order * before) / (order + 1)
        before = current
        current = after
    return (current, before)


def gll_derivative(points_n):
    degree = points_n - 1
    points = []
    for index in range(points_n):
        point = -math.cos(math.pi * index / degree)
        for sweep in range(100):
            top_val, below_val = legendre_values(degree, point)
            point = point - (point * top_val - below_val) / (points_n * top_val)
        points.append(point)
    values = [legendre_values(degree, point)[0] for point in points]
    rows = [
        [
            0.0 if r == c else values[r] / (values[c] * (points[r] - points[c]))
            for c in range(points_n)
        ]
        for r in range(points_n)
    ]
    rows[0][0] = -degree * (degree + 1) / 4.0
    rows[degree][degree] = degree * (degree + 1) / 4.0
    return np.asarray(rows, np.float32)


def plane_tables():
    plane = np.arange(PLANES)
    wave = plane // 2
    phase = (plane[:, None] * wave[None, :] % PLANES) * (2.0 * math.pi / PLANES)
    synth = np.where(plane[None, :] % 2 == 1, np.sin(phase), np.cos(phase))
    synth[:, 1] = 1 - 2 * (plane % 2)
    scales = np.where(wave == 0, 1.0 / PLANES, 2.0 / PLANES)
    analysis = synth.T * scales[:, None]
    number = wave * (2.0 / PLANES)
    axial = np.zeros((PLANES, PLANES))
    axial[plane[::2], plane[1::2]] = number[::2]
    axial[plane[1::2], plane[::2]] = -number[1::2]
    both = np.concatenate([synth, synth @ axial])
    return both.astype(np.float32), (STEP_SIZE * analysis).astype(np.float32)


def step_kernel(
    u_ref, base_ref, geo_ref, mass_ref, synth_ref, anal_ref, table_ref,
    ut, along, rows, slopes, base, stage, inputs, fields, forcing, back, returned, table,
    row_send, relay_send, slope_send, back_send, row_recv, slope_recv, back_recv,
    own_sem, stage_sem, table_sem,
):
    deriv = gll_derivative(NP)
    me = lax.axis_index("four")
    x, z = me // 8, me % 8
    odd = z % 2
    sign = 1 - 2 * odd
    partner = x * 8 + z + sign

    def remote(src, dst, send, recv, to):
        return pltpu.make_async_remote_copy(
            src_ref=src, dst_ref=dst, send_sem=send, recv_sem=recv,
            device_id={"four": to}, device_id_type=MESH,
        )

    def source(dx, k):
        return ((x + dx) % 2) * 8 + (z - sign * k + 8) % 8

    def target(dx, k):
        off = (0, 2, -1, -3)[k]
        return ((x + dx) % 2) * 8 + (z + sign * off + 8) % 8

    def pair(dev):
        return pl.multiple_of((dev // 2) * 8, 8)

    def stage_copy(f):
        return pltpu.make_async_copy(base_ref.at[f], stage.at[f % 2], stage_sem.at[f % 2])

    def turn(h):
        def block(t, _):
            c = t // 8
            i = pl.multiple_of((t % 8) * 8, 8)
            ut[h, c, pl.ds(i, 8)] = jnp.swapaxes(u_ref[c, :, pl.ds(i, 8), pl.ds(h * LANES, LANES)], 0, 1)
            return 0
        lax.fori_loop(0, 24, block, 0)

    def differentiate(h):
        def block(t, _):
            c, j = t // 8, t % 8
            vals = [ut[h, c, 8 * i + j] for i in range(8)]
            for i in range(8):
                total = vals[0] * float(deriv[i, 0])
                for k in range(1, 8):
                    total = total + vals[k] * float(deriv[i, k])
                along[h, c, 8 * i + j] = total
            return 0
        lax.fori_loop(0, 24, block, 0)

    def row_copy(h, dx, k):
        to = target(dx, k)
        return remote(ut.at[h, :, pl.ds(pair(to), 8)], rows.at[h, me], row_send.at[h, dx * 4 + k], row_recv.at[h, me], to)

    def own_relay(h):
        return remote(ut.at[h, :, pl.ds(pair(me), 8)], rows.at[h, me], relay_send.at[h, 0], row_recv.at[h, me], partner)

    def relay(h, dx, k):
        src = source(dx, k)
        return remote(rows.at[h, src], rows.at[h, src], relay_send.at[h, dx * 4 + k], row_recv.at[h, src], partner)

    def far_source(dx, k):
        return ((x + dx) % 2) * 8 + (z + sign + sign * k + 8) % 8

    def row_wait(h, src):
        remote(rows.at[h, src], rows.at[h, src], relay_send.at[h, 0], row_recv.at[h, src], partner).wait_recv()

    def slope_copy(h, t):
        to = (me + t) % GROUP
        return remote(
            along.at[h, :, pl.ds(to * 4, 4)], slopes.at[h, me], slope_send.at[h, t], slope_recv.at[h, me], to
        )

    def slope_wait(h, t):
        src = (me + t) % GROUP
        remote(slopes.at[h, src], slopes.at[h, src], slope_send.at[h, t], slope_recv.at[h, src], src).wait_recv()

    def back_copy(h, t):
        to = (me + t) % GROUP
        return remote(back.at[h, to], returned.at[h, me], back_send.at[h, t], back_recv.at[h, me], to)

    def back_wait(h, src):
        remote(returned.at[h, src], returned.at[h, src], back_send.at[h, 0], back_recv.at[h, src], partner).wait_recv()

    def own_copies(h):
        return (
            pltpu.make_async_copy(ut.at[h, :, pl.ds(pair(me), 8)], rows.at[h, me], own_sem.at[h, 0]),
            pltpu.make_async_copy(along.at[h, :, pl.ds(me * 4, 4)], slopes.at[h, me], own_sem.at[h, 1]),
        )

    def own_back(h):
        return pltpu.make_async_copy(back.at[h, me], returned.at[h, me], own_sem.at[h, 2])

    NEAR = [(1, 0), (0, 1), (1, 1), (0, 2), (1, 2), (0, 3), (1, 3)]
    SENT = [(0, 3), (1, 3), (0, 1), (1, 1), (0, 2), (1, 2), (1, 0)]

    def each(fn):
        def go(t, _):
            fn(t)
            return 0
        lax.fori_loop(1, GROUP, go, 0)

    def send_rows(h):
        for dx, k in SENT:
            row_copy(h, dx, k).start()
        own_relay(h).start()

    def send_slopes(h):
        each(lambda t: slope_copy(h, t).start())

    def relays(h):
        for dx, k in NEAR:
            row_wait(h, source(dx, k))
            relay(h, dx, k).start()

    def compute(h):
        for copy in own_copies(h):
            copy.wait()
        for k in range(4):
            for dx in range(2):
                row_wait(h, far_source(dx, k))
        each(lambda t: slope_wait(h, t))

        def gather(s, _):
            at = pl.ds(pl.multiple_of(s * COEFS, COEFS), COEFS)
            for c in range(3):
                line = [rows[h, s, c, j] for j in range(8)]
                for n in range(4):
                    total = None
                    for k in range(8):
                        term = line[k] * jnp.where(odd == 1, float(deriv[4 + n, k]), float(deriv[n, k]))
                        total = term if total is None else total + term
                    inputs[n, at, pl.ds(c * LANES, LANES)] = jnp.where(odd == 1, line[4 + n], line[n])
                    inputs[n, at, pl.ds((3 + c) * LANES, LANES)] = total
                    inputs[n, at, pl.ds((6 + c) * LANES, LANES)] = slopes[h, s, c, n]
            return 0
        lax.fori_loop(0, GROUP, gather, 0)

        def node(n, _):
            fields[:, 0 : 9 * LANES] = jnp.dot(
                synth_ref[0:PLANES], inputs[n], precision=HIGH, preferred_element_type=jnp.float32
            )
            fields[:, 9 * LANES : 12 * LANES] = jnp.dot(
                synth_ref[PLANES : 2 * PLANES], inputs[n, :, 0 : 3 * LANES],
                precision=HIGH, preferred_element_type=jnp.float32,
            )
            geo = [geo_ref[g, n, :, pl.ds(h * LANES, LANES)] for g in range(4)]

            def planes(p, _):
                at = pl.ds(pl.multiple_of(p * 16, 16), 16)
                flow = [base[f, n, at, pl.ds(h * LANES, LANES)].astype(jnp.float32) for f in range(12)]
                get = lambda f: fields[at, f * LANES : (f + 1) * LANES]
                on_r = flow[0] * geo[0] + flow[1] * geo[2]
                on_s = flow[0] * geo[1] + flow[1] * geo[3]
                vel = [get(c) for c in range(3)]
                for c in range(3):
                    total = vel[0] * flow[3 + 3 * c] + vel[1] * flow[4 + 3 * c] + vel[2] * flow[5 + 3 * c]
                    total = total - on_r * get(6 + c) - on_s * get(3 + c) - flow[2] * get(9 + c)
                    forcing[at, c * LANES : (c + 1) * LANES] = total
                return 0
            lax.fori_loop(0, PLANES // 16, planes, 0)
            modes = jnp.dot(anal_ref[...], forcing[...], precision=HIGH, preferred_element_type=jnp.float32)
            for c in range(3):
                back[h, :, c, n] = modes[:, c * LANES : (c + 1) * LANES].reshape(GROUP, COEFS, LANES)
            return 0
        lax.fori_loop(0, 4, node, 0)

    def table_copy(h, s):
        at = pl.ds(pl.multiple_of((h * NODES + 4 * s) * LANES, 4 * LANES), 4 * LANES)
        return pltpu.make_async_copy(table.at[at], table_ref.at[at], table_sem.at[h, s])

    def finish(h, s):
        for n in range(4):
            at = 4 * s + n
            weight = mass_ref[at, :, pl.ds(h * LANES, LANES)]
            parts = [(ut[h, c, at] + returned[h, s, c, n]) * weight for c in range(3)]
            parts.append(jnp.broadcast_to(weight, (8, LANES)))
            parts.append(jnp.zeros((128 - 56, LANES), jnp.float32))
            begin = pl.multiple_of((h * NODES + at) * LANES, LANES)
            table[pl.ds(begin, LANES)] = jnp.concatenate(parts).T
        table_copy(h, s).start()

    stage_copy(0).start()
    stage_copy(1).start()
    barrier = pltpu.get_barrier_semaphore()
    each(lambda t: pl.semaphore_signal(barrier, inc=1, device_id={"four": (me + t) % GROUP}, device_id_type=MESH))
    turn(0)
    pl.semaphore_wait(barrier, GROUP - 1)
    send_rows(0)
    differentiate(0)
    send_slopes(0)
    for copy in own_copies(0):
        copy.start()
    turn(1)
    differentiate(1)
    for copy in own_copies(1):
        copy.start()

    for f in range(12):
        stage_copy(f).wait()

        def move(t, _):
            p = pl.multiple_of(t * 64, 64)
            block = stage[f % 2, pl.ds(p, 64)].astype(jnp.float32)
            base[f, :, pl.ds(p, 64), :] = jnp.swapaxes(block, 0, 1).astype(jnp.bfloat16)
            return 0
        lax.fori_loop(0, 4, move, 0)
        if f + 2 < 12:
            stage_copy(f + 2).start()

    relays(0)
    send_rows(1)
    send_slopes(1)
    compute(0)
    own_back(0).start()
    relays(1)
    each(lambda t: back_copy(0, t).start())
    compute(1)
    own_back(1).start()
    each(lambda t: back_copy(1, t).start())

    for h in range(HALVES):
        own_back(h).wait()
        finish(h, me)

        def arrive(t, _):
            src = (me + t) % GROUP
            back_wait(h, src)
            finish(h, src)
            return 0
        lax.fori_loop(1, GROUP, arrive, 0)

    for h in range(HALVES):
        for dx, k in SENT:
            row_copy(h, dx, k).wait_send()
        own_relay(h).wait_send()
        for dx, k in NEAR:
            relay(h, dx, k).wait_send()
        each(lambda t: slope_copy(h, t).wait_send())
        each(lambda t: back_copy(h, t).wait_send())

        def drained(s, _):
            table_copy(h, s).wait()
            return 0
        lax.fori_loop(0, GROUP, drained, 0)


def step(u, base, geo, mass):
    synth, anal = plane_tables()
    vmem = pl.BlockSpec(memory_space=pltpu.VMEM)
    hbm = pl.BlockSpec(memory_space=pl.ANY)
    f32 = jnp.float32
    dma = pltpu.SemaphoreType.DMA
    return pl.pallas_call(
        step_kernel,
        out_shape=jax.ShapeDtypeStruct((POINTS, 128), f32),
        in_specs=[vmem, hbm, vmem, vmem, vmem, vmem],
        out_specs=hbm,
        scratch_shapes=[
            pltpu.VMEM((HALVES, 3, NODES, COEFS, LANES), f32),
            pltpu.VMEM((HALVES, 3, NODES, COEFS, LANES), f32),
            pltpu.VMEM((HALVES, GROUP, 3, 8, COEFS, LANES), f32),
            pltpu.VMEM((HALVES, GROUP, 3, 4, COEFS, LANES), f32),
            pltpu.VMEM((12, 4, PLANES, E_DEV), jnp.bfloat16),
            pltpu.VMEM((2, PLANES, 4, E_DEV), jnp.bfloat16),
            pltpu.VMEM((4, PLANES, 9 * LANES), f32),
            pltpu.VMEM((PLANES, 12 * LANES), f32),
            pltpu.VMEM((PLANES, 3 * LANES), f32),
            pltpu.VMEM((HALVES, GROUP, 3, 4, COEFS, LANES), f32),
            pltpu.VMEM((HALVES, GROUP, 3, 4, COEFS, LANES), f32),
            pltpu.VMEM((POINTS, 128), f32),
            dma((HALVES, 8)), dma((HALVES, 8)), dma((HALVES, GROUP)), dma((HALVES, GROUP)),
            dma((HALVES, GROUP)), dma((HALVES, GROUP)), dma((HALVES, GROUP)),
            dma((HALVES, 3)), dma((2,)), dma((HALVES, GROUP)),
        ],
        compiler_params=pltpu.CompilerParams(
            collective_id=0, has_side_effects=True, vmem_limit_bytes=VMEM_LIMIT
        ),
        name="step",
    )(u, base, geo, mass, jnp.asarray(synth), jnp.asarray(anal))


def lists_block(n, ids_ref, state):
    counts, firsts, lists, used = state
    bf, f32 = jnp.bfloat16, jnp.float32
    width = E_DEV

    def iota(shape, dim):
        return lax.broadcasted_iota(jnp.int32, shape, dim)

    def flat(left, right):
        return lax.dot_general(left, right, (((1,), (1,)), ((), ())), preferred_element_type=f32)

    ids = ids_ref[n]
    digit = iota((128, width), 0)
    high = (digit == ids // 128).astype(bf)
    low = (digit == ids % 128).astype(bf)
    prior = jnp.sum(low.astype(f32) * jnp.dot(counts[...].astype(bf), high, preferred_element_type=f32), axis=0, keepdims=True)
    across = jnp.broadcast_to(ids.astype(f32), (width, width))
    same = jnp.where((across == across.T) & (iota((width, width), 0) < iota((width, width), 1)), 1.0, 0.0)
    again = jnp.where(prior + jnp.sum(same, axis=0, keepdims=True) > 0, 1.0, 0.0)
    counts[...] = counts[...] + flat(low, high)
    lane = iota((1, width), 1)
    block = ((lane // LANES) * NODES + n).astype(f32)
    inner = (lane % LANES).astype(f32)
    once = 1.0 - again
    low_f = low.astype(f32)
    firsts[...] = firsts[...] + flat(
        jnp.concatenate([low_f * (once * block), low_f * (once * inner)]).astype(bf), high
    )
    found = jnp.dot(firsts[...].astype(bf), high, preferred_element_type=f32)
    rep_block = jnp.sum(found[0:128] * low_f, axis=0, keepdims=True)
    rep_inner = jnp.sum(found[128:256] * low_f, axis=0, keepdims=True)
    before = jnp.dot(
        jnp.broadcast_to(again, (8, width)).astype(bf),
        jnp.where(iota((width, width), 0) < iota((width, width), 1), 1.0, 0.0).astype(bf),
        preferred_element_type=f32,
    )[0:1]
    slot = (before + used[0:1, 0:1]).astype(jnp.int32)
    used[...] = used[...] + jnp.sum(again, axis=1, keepdims=True)
    slot_low = jnp.where(digit == slot % 128, again, 0.0)
    slot_high = (digit == slot // 128).astype(bf)
    left = jnp.concatenate([slot_low * v for v in (block, inner, rep_block, rep_inner)]).astype(bf)
    lists[...] = lists[...] + flat(left, slot_high)


def lists_start(state):
    for ref in state:
        ref[...] = jnp.zeros_like(ref)


def lists_end(rim_ref, state, place_ref, rep_ref, rim_at_ref):
    counts, firsts, lists, used = state
    bf, f32 = jnp.bfloat16, jnp.float32
    index = lax.broadcasted_iota(jnp.int32, (128, 128), 0) * 128 + lax.broadcasted_iota(jnp.int32, (128, 128), 1)
    for k, ref in enumerate((place_ref, rep_ref)):
        at = lists[256 * k : 256 * k + 128] * 128.0 + lists[256 * k + 128 : 256 * k + 256]
        ref[...] = jnp.where(index < EXTRA, at.T.astype(jnp.int32), POINTS)[0:LIST_ROWS]
    rim = rim_ref[...]
    digit = lax.broadcasted_iota(jnp.int32, (128, RIM_PAD), 0)
    high = (digit == rim // 128).astype(bf)
    low = (digit == rim % 128).astype(f32)
    found = jnp.dot(firsts[...].astype(bf), high, preferred_element_type=f32)
    rep_block = jnp.sum(found[0:128] * low, axis=0, keepdims=True)
    rep_inner = jnp.sum(found[128:256] * low, axis=0, keepdims=True)
    rim_at_ref[...] = (rep_block * 128.0 + rep_inner).astype(jnp.int32)


def lists_kernel(ids_ref, rim_ref, place_ref, rep_ref, rim_at_ref, *state):
    lists_start(state)

    def go(n, _):
        lists_block(n, ids_ref, state)
        return 0
    lax.fori_loop(0, NODES, go, 0)
    lists_end(rim_ref, state, place_ref, rep_ref, rim_at_ref)


LIST_STATE = [
    pltpu.VMEM((128, 128), jnp.float32),
    pltpu.VMEM((256, 128), jnp.float32),
    pltpu.VMEM((512, 128), jnp.float32),
    pltpu.VMEM((8, 128), jnp.float32),
]
LIST_SHAPES = (
    jax.ShapeDtypeStruct((LIST_ROWS, 128), jnp.int32),
    jax.ShapeDtypeStruct((LIST_ROWS, 128), jnp.int32),
    jax.ShapeDtypeStruct((1, RIM_PAD), jnp.int32),
)


def node_lists(connect, edges):
    vmem = pl.BlockSpec(memory_space=pltpu.VMEM)
    rim = jnp.pad(edges.reshape(1, -1), ((0, 0), (0, RIM_PAD - 2 * RIM)))
    return pl.pallas_call(
        lists_kernel,
        out_shape=LIST_SHAPES,
        in_specs=[vmem] * 2,
        out_specs=(vmem,) * 3,
        scratch_shapes=LIST_STATE,
        compiler_params=pltpu.CompilerParams(vmem_limit_bytes=VMEM_LIMIT),
        name="lists",
    )(connect.reshape(NODES, 1, E_DEV), rim)


def gather_kernel(place_ref, rep_ref, rim_ref, table_ref, summed_ref, rims_ref, table, sems):
    load = pltpu.make_async_copy(table_ref, table.at[pl.ds(0, POINTS)], sems.at[0])
    load.start()
    table[pl.ds(POINTS, 8)] = jnp.zeros((8, 128), jnp.float32)
    load.wait()

    def add(t, _):
        for k in range(8):
            at = pl.ds(rep_ref[t // 16, (t % 16) * 8 + k], 1)
            table[at] = table[at] + table[pl.ds(place_ref[t // 16, (t % 16) * 8 + k], 1)]
        return 0
    lax.fori_loop(0, (EXTRA + 7) // 8, add, 0)
    store = pltpu.make_async_copy(table.at[pl.ds(0, POINTS)], summed_ref, sems.at[0])
    store.start()

    def pick(t, _):
        for k in range(9):
            rims_ref[pl.ds(t * 9 + k, 1)] = table[pl.ds(rim_ref[0, t * 9 + k], 1)]
        return 0
    lax.fori_loop(0, 2 * RIM // 9, pick, 0)
    store.wait()


def spread_kernel(place_ref, rep_ref, rim_ref, summed_ref, lower_ref, upper_ref, out_ref, table, sems):
    load = pltpu.make_async_copy(summed_ref, table.at[pl.ds(0, POINTS)], sems.at[0])
    load.start()
    table[pl.ds(POINTS, 8)] = jnp.zeros((8, 128), jnp.float32)
    load.wait()

    def add(t, _):
        for k in range(9):
            at = pl.ds(rim_ref[0, t * 9 + k], 1)
            table[at] = table[at] + lower_ref[pl.ds(t * 9 + k, 1)]
        for k in range(9):
            at = pl.ds(rim_ref[0, RIM + t * 9 + k], 1)
            table[at] = table[at] + upper_ref[pl.ds(t * 9 + k, 1)]
        return 0
    lax.fori_loop(0, RIM // 9, add, 0)

    def spread(t, _):
        vals = [table[pl.ds(rep_ref[t // 16, (t % 16) * 8 + k], 1)] for k in range(8)]
        for k in range(8):
            table[pl.ds(place_ref[t // 16, (t % 16) * 8 + k], 1)] = vals[k]
        return 0
    lax.fori_loop(0, (EXTRA + 7) // 8, spread, 0)

    def write(t, _):
        h, i = t // 8, t % 8
        parts = []
        for j in range(8):
            begin = pl.multiple_of((h * NODES + i * 8 + j) * LANES, LANES)
            cols = table[pl.ds(begin, LANES)].T
            parts.append(cols[0:48] / cols[48:49])
        block = jnp.swapaxes(jnp.stack(parts), 0, 1)
        out_ref[:, pl.ds(pl.multiple_of(i * 8, 8), 8), pl.ds(pl.multiple_of(h * LANES, LANES), LANES)] = block
        return 0
    lax.fori_loop(0, 16, write, 0)


def assemble(table, connect, edges):
    place, rep, rim_at = node_lists(connect, edges)
    smem = pl.BlockSpec(memory_space=pltpu.SMEM)
    vmem = pl.BlockSpec(memory_space=pltpu.VMEM)
    hbm = pl.BlockSpec(memory_space=pl.ANY)
    f32 = jnp.float32
    params = pltpu.CompilerParams(vmem_limit_bytes=VMEM_LIMIT)
    scratch = [pltpu.VMEM((POINTS + 8, 128), f32), pltpu.SemaphoreType.DMA((1,))]
    summed, rims = pl.pallas_call(
        gather_kernel,
        out_shape=(jax.ShapeDtypeStruct((POINTS, 128), f32), jax.ShapeDtypeStruct((2 * RIM, 128), f32)),
        in_specs=[smem, smem, smem, hbm],
        out_specs=(hbm, vmem),
        scratch_shapes=scratch,
        compiler_params=params,
        name="gather",
    )(place, rep, rim_at, table.reshape(POINTS, 128))
    count = lax.axis_size("mesh")
    up = [(i, (i + 1) % count) for i in range(count)]
    down = [(j, i) for i, j in up]
    from_lower = lax.ppermute(rims[RIM:], "mesh", up)
    from_upper = lax.ppermute(rims[:RIM], "mesh", down)
    return pl.pallas_call(
        spread_kernel,
        out_shape=jax.ShapeDtypeStruct((3 * COEFS, NODES, E_DEV), f32),
        in_specs=[smem, smem, smem, hbm, vmem, vmem],
        out_specs=vmem,
        scratch_shapes=scratch,
        compiler_params=params,
        name="spread",
    )(place, rep, rim_at, summed, from_lower, from_upper)


def body(adj_modes, base_flow, geometry, mass, connect, edge_nodes):
    me = lax.axis_index("four")
    geo = lax.dynamic_slice_in_dim(geometry, me * 4, 4, 1).reshape(4, 4, 1, E_DEV)
    table = step(adj_modes, base_flow, geo, mass.reshape(NODES, 1, E_DEV))
    out = assemble(table, connect, edge_nodes[0])
    return out.reshape(adj_modes.shape)


def solution(mesh):
    return jax.shard_map(
        body,
        mesh=mesh,
        in_specs=(
            P(None, "four", None, "mesh"),
            P(None, None, "four", "mesh"),
            P(None, None, "mesh"),
            P(None, "mesh"),
            P(None, "mesh"),
            P("mesh", None, None),
        ),
        out_specs=P(None, "four", None, "mesh"),
        check_vma=False,
    )
```

time: 671 us -> 377 us (0.56); the launches traced: 663 us -> 376 us
  Pallas kernels: 0 us -> 357 us
  waiting for transfers between devices: 315 us -> 7.87 us
  local copies, waits for them, and re-layouts: 153 us -> 6.65 us
  other arithmetic: 124 us -> 0 us
  matrix products: 37.1 us -> 0 us
  starting transfers between devices: 33.2 us -> 4.03 us
    pallas_call x0 -> x4, Pallas kernels: none -> 357 us  [the longest x1 252 us: step(): pl.pallas_call(step_kernel, out_shape=jax.ShapeDtypeStruct((POINTS, 128),...]
    all_to_all x2 -> x0, waiting for transfers between devices: 315 us -> none  [the longest x1 245 us: body(): lax.all_to_all(packed, 'four', split_axis=2, concat_axis=1, tiled=True)]
    scatter-add x1 -> x0, other arithmetic: 90.8 us -> none  [assemble(): jnp.zeros((rows.shape[0], UNIQUE), jnp.float32).at[:, node_ids].add(rows)]
    gather x4 -> x0, local copies, waits for them, and re-layouts: 71.2 us -> none  [the longest x2 64 us: assemble(): spread_back = summed[:, node_ids]]
    dot_general x4 -> x0, matrix products: 37.1 us -> none  [the longest x1 24.3 us: body(): physical = jnp.einsum('jm,fmne->fjne', synth, spread, precision=HIGH)]
    unnamed x48 -> x6, local copies, waits for them, and re-layouts: 31.4 us -> 0.64 us
    all_to_all x2 -> x0, starting transfers between devices: 27.4 us -> none  [the longest x1 17.1 us: body(): lax.all_to_all(forcing_modes, 'four', split_axis=1, concat_axis=2, tiled=...]
    concatenate x2 -> x0, local copies, waits for them, and re-layouts: 23.2 us -> none  [the longest x1 16.3 us: body(): packed = jnp.concatenate([adj_modes, grad_x, grad_y, grad_z])]
  transfers between devices with their start and end apart: 4 -> 2, of which waited for: 2 -> 2; matrix products, arithmetic and copies ran while one was open for 7% -> 0% of each run, Pallas kernels for 0% -> 0%
where the time goes in v1:
time: 377 us; the launch traced here: 376 us
  Pallas kernels  357 us (95%)
  waiting for transfers between devices  7.87 us (2%)
  local copies, waits for them, and re-layouts  6.65 us (2%)
  starting transfers between devices  4.03 us (1%)
    pallas_call x1, Pallas kernels, step(): pl.pallas_call(step_kernel, out_shape=jax.ShapeDtypeStruct((POINTS, 128),...  252 us
    pallas_call x1, Pallas kernels, node_lists(): pl.pallas_call(lists_kernel, out_shape=LIST_SHAPES, in_specs=[vmem] * 2,...  52.6 us
    pallas_call x1, Pallas kernels, assemble(): pl.pallas_call(gather_kernel, out_shape=(jax.ShapeDtypeStruct((POINTS, 12...  26.8 us
    pallas_call x1, Pallas kernels, assemble(): pl.pallas_call(spread_kernel, out_shape=jax.ShapeDtypeStruct((3 * COEFS,...  26.4 us
  transfers between devices with their start and end apart: 2, of which 2 were waited for; matrix products, arithmetic and copies ran while one was open for 0% of the time, Pallas kernels for 0%

profile of v1, /device:TPU:2, one launch (start us, length us, event | category | flops | bytes accessed | tf_op | source)
XLA Modules:
  0.0 376.0 jit_solution(11560829688978533234)
XLA Ops:
  0.0 0.0 copy-start
  0.0 0.8 reshape_squeeze.3
  0.8 0.6 pad.4.rim_ref
  1.4 0.0 copy-done
  1.4 0.6 reshape.13.geo_ref
  2.0 1.5 reshape.14.mass_ref
  3.5 1.5 reshape.12.ids_ref
  5.0 52.6 %lists.1 = (s32[32,128]{1,0:T(8,128)}, s32[32,128]{1,0:T(8,128)}, s32[1,512]{1,0:T(1,128)}) custom-call(s32[64,1,256]{2,1,0:T(1,128)} %reshape.12.ids_ref, s32[1,512]{1,0:T(1,128)} %pad.4.rim_ref), custom_call_target="tpu_custom_call" | custom-call | tf_op jit(solution)/shard_map/lists/pallas_call | solution.py:456
  57.6 251.6 %step.1.table_ref = f32[16384,128]{1,0:T(8,128)} custom-call(f32[3,16,64,256]{3,2,1,0:T(8,128)} %u_ref.1, bf16[12,256,4,256]{3,2,1,0:T(4,128)(2,1)} %base_ref.1, f32[4,4,1,256]{3,2,1,0:T(1,128)} %reshape.13.geo_ref, f32[64,1,256]{2,1,0:T(1,128)} %reshape.14.mass_ref, f32[512,256]{1,0:T(8,128)} %constant.14.clone.synth_ref, f32[256,256]{1,0:T(8,128)} %constant.15.clone.anal_ref), custom_call_target="tpu_custom_call" | custom-call | tf_op jit(solution)/shard_map/step/pallas_call | solution.py:335
  309.3 26.8 %gather.1 = (f32[16384,128]{1,0:T(8,128)}, f32[450,128]{1,0:T(8,128)}) custom-call(s32[32,128]{1,0:T(8,128)} %get-tuple-element.10.place_ref, s32[32,128]{1,0:T(8,128)} %get-tuple-element.11.rep_ref, s32[1,512]{1,0:T(1,128)} %get-tuple-element.12.rim_ref, f32[16384,128]{1,0:T(8,128)} %step.1.table_ref), custom_call_target="tpu_custom_call" | custom-call | tf_op jit(solution)/shard_map/gather/pallas_call | solution.py:534
  336.1 1.0 fusion
  337.1 4.0 %collective-permute-start.1 = (f32[225,128]{1,0:T(8,128)S(1)}, f32[225,128]{1,0:T(8,128)S(1)}, u32[]{:S(2)}, u32[]{:S(2)}) collective-permute-start(f32[225,128]{1,0:T(8,128)S(1)} %get-tuple-element.15), channel_id=1, source_target_pairs={{16,0},{32,16},{48,32},{64,48},{80,64},{96,80},{112,96},{128,112},... | collective-permute-start | bytes 345608 | tf_op jit(solution)/shard_map/ppermute | solution.py:547
  341.1 0.0 collective-permute-start
  341.1 2.4 collective-permute-done.1.upper_ref
  343.5 0.0 copy-start.1
  343.5 5.5 %collective-permute-done.lower_ref = f32[225,128]{1,0:T(8,128)S(1)} collective-permute-done((f32[225,128]{1,0:T(8,128)S(1)}, f32[225,128]{1,0:T(8,128)S(1)}, u32[]{:S(2)}, u32[]{:S(2)}) %collective-permute-start) | collective-permute-done | bytes 115232 | tf_op jit(solution)/shard_map/ppermute | solution.py:546
  349.0 0.0 copy-start.2
  349.0 0.0 copy-done.1
  349.0 0.6 copy-done.2
  349.6 26.4 %spread.1 = f32[48,64,256]{2,1,0:T(8,128)} custom-call(s32[32,128]{1,0:T(8,128)} %get-tuple-element.10.place_ref, s32[32,128]{1,0:T(8,128)} %get-tuple-element.11.rep_ref, s32[1,512]{1,0:T(1,128)} %get-tuple-element.12.rim_ref, f32[16384,128]{1,0:T(8,128)} %get-tuple-element.13.summed_ref, f32[225,128]{1,0:T(8,128)} %copy-done.2, f32[225,128]{1,0:T(8,128)} %copy-done.1), custom_call_target="tpu_custom_call" | custom-call | tf_op jit(solution)/shard_map/spread/pallas_call | solution.py:548
  (1 shorter events, 0.0 us)
Async XLA Ops:
  0.0 1.4 copy-start
  337.1 6.4 %collective-permute-start.1 = (f32[225,128]{1,0:T(8,128)S(1)}, f32[225,128]{1,0:T(8,128)S(1)}, u32[]{:S(2)}, u32[]{:S(2)}) collective-permute-start(f32[225,128]{1,0:T(8,128)S(1)} %get-tuple-element.15), channel_id=1, source_target_pairs={{16,0},{32,16},{48,32},{64,48},{80,64},{96,80},{112,96},{128,112},... | collective-permute-start | bytes 345608 | tf_op jit(solution)/shard_map/ppermute | solution.py:547
  341.1 7.9 %collective-permute-start = (f32[225,128]{1,0:T(8,128)S(1)}, f32[225,128]{1,0:T(8,128)S(1)}, u32[]{:S(2)}, u32[]{:S(2)}) collective-permute-start(f32[225,128]{1,0:T(8,128)S(1)} %get-tuple-element.16), channel_id=1, source_target_pairs={{0,16},{16,32},{32,48},{48,64},{64,80},{80,96},{96,112},{112,128},... | collective-permute-start | bytes 345608 | tf_op jit(solution)/shard_map/ppermute | solution.py:546
  343.5 5.5 %copy-start.1 = (f32[225,128]{1,0:T(8,128)}, f32[225,128]{1,0:T(8,128)S(1)}, u32[]{:S(2)}) copy-start(f32[225,128]{1,0:T(8,128)S(1)} %collective-permute-done.1.upper_ref) | copy-start | bytes 345604
  349.0 0.6 copy-start.2

commit v2 on v1

--- a/solution.py
+++ b/solution.py
@@ -16,11 +16,14 @@
 E_DEV = 256
 POINTS = NODES * E_DEV
 EXTRA = POINTS - UNIQUE
-LIST_ROWS = (EXTRA + 1023) // 1024 * 8
+BATCH = 8
+LISTED = (EXTRA + BATCH + 127) // 128 * 128
+LIST_ROWS = (LISTED // 128 + 8) // 8 * 8
 RIM = 225
-RIM_PAD = 512
+RIM_PAD = 256
 HALVES = 2
 LANES = E_DEV // HALVES
+N_MESH = 16
 GROUP = 16
 COEFS = PLANES // GROUP
 STEP_SIZE = 0.1
@@ -78,10 +81,11 @@
 
 
 def step_kernel(
-    u_ref, base_ref, geo_ref, mass_ref, synth_ref, anal_ref, table_ref,
+    u_ref, base_ref, geometry_ref, mass_ref, ids_ref, rim_ref, synth_ref, anal_ref,
+    table_ref, place_ref, rep_ref, rim_at_ref, rims_ref,
     ut, along, rows, slopes, base, stage, inputs, fields, forcing, back, returned, table,
     row_send, relay_send, slope_send, back_send, row_recv, slope_recv, back_recv,
-    own_sem, stage_sem, table_sem,
+    own_sem, stage_sem, table_sem, geo, rim_ids, rims, met, rim_send, rim_recv, *lists_state,
 ):
     deriv = gll_derivative(NP)
     me = lax.axis_index("four")
@@ -225,14 +229,14 @@
                 synth_ref[PLANES : 2 * PLANES], inputs[n, :, 0 : 3 * LANES],
                 precision=HIGH, preferred_element_type=jnp.float32,
             )
-            geo = [geo_ref[g, n, :, pl.ds(h * LANES, LANES)] for g in range(4)]
+            metric = [geo[g, n, :, pl.ds(h * LANES, LANES)] for g in range(4)]
 
             def planes(p, _):
                 at = pl.ds(pl.multiple_of(p * 16, 16), 16)
                 flow = [base[f, n, at, pl.ds(h * LANES, LANES)].astype(jnp.float32) for f in range(12)]
                 get = lambda f: fields[at, f * LANES : (f + 1) * LANES]
-                on_r = flow[0] * geo[0] + flow[1] * geo[2]
-                on_s = flow[0] * geo[1] + flow[1] * geo[3]
+                on_r = flow[0] * metric[0] + flow[1] * metric[2]
+                on_s = flow[0] * metric[1] + flow[1] * metric[3]
                 vel = [get(c) for c in range(3)]
                 for c in range(3):
                     total = vel[0] * flow[3 + 3 * c] + vel[1] * flow[4 + 3 * c] + vel[2] * flow[5 + 3 * c]
@@ -250,23 +254,66 @@
         at = pl.ds(pl.multiple_of((h * NODES + 4 * s) * LANES, 4 * LANES), 4 * LANES)
         return pltpu.make_async_copy(table.at[at], table_ref.at[at], table_sem.at[h, s])
 
+    def four_rows(block, s):
+        return jnp.where(s % 2 == 1, block[4:8], block[0:4])
+
+    def rim_start():
+        for k in range(2):
+            row = jnp.concatenate([rim_ref[0, k : k + 1], jnp.full((1, RIM_PAD - RIM), -1, jnp.int32)], axis=1)
+            rim_ids[k * RIM_PAD : (k + 1) * RIM_PAD] = jnp.broadcast_to(row.astype(jnp.float32), (128, RIM_PAD)).T
+        rims[...] = jnp.zeros_like(rims)
+
+    def rim_sums(h, s, ids):
+        at = pl.ds(pl.multiple_of((h * NODES + 4 * s) * LANES, 4 * LANES), 4 * LANES)
+        rest = table[at, 0:LANES]
+        pieces = []
+        for _ in range(3):
+            pieces.append(rest.astype(jnp.bfloat16))
+            rest = rest - pieces[-1].astype(jnp.float32)
+        hit = jnp.concatenate(
+            [(rim_ids[...] == ids[n : n + 1].astype(jnp.float32)).astype(jnp.bfloat16) for n in range(4)], axis=1
+        )
+        sums = jnp.dot(hit, jnp.concatenate(pieces, axis=1), preferred_element_type=jnp.float32)
+        rims[...] = rims[...] + (sums[:, 0:128] + (sums[:, 128:256] + sums[:, 256:384]))
+
+    def rim_copy(side):
+        to = (lax.axis_index("mesh") + (N_MESH - 1 if side == 0 else 1)) % N_MESH
+        return pltpu.make_async_remote_copy(
+            src_ref=rims.at[pl.ds(side * RIM_PAD, RIM_PAD)], dst_ref=met.at[pl.ds((1 - side) * RIM_PAD, RIM_PAD)],
+            send_sem=rim_send.at[side], recv_sem=rim_recv.at[1 - side],
+            device_id={"mesh": to}, device_id_type=MESH,
+        )
+
     def finish(h, s):
+        tile = pl.ds(pl.multiple_of((s // 2) * 8, 8), 8)
+        weights = four_rows(mass_ref[tile, pl.ds(h * LANES, LANES)], s)
         for n in range(4):
             at = 4 * s + n
-            weight = mass_ref[at, :, pl.ds(h * LANES, LANES)]
+            weight = weights[n : n + 1]
             parts = [(ut[h, c, at] + returned[h, s, c, n]) * weight for c in range(3)]
             parts.append(jnp.broadcast_to(weight, (8, LANES)))
             parts.append(jnp.zeros((128 - 56, LANES), jnp.float32))
             begin = pl.multiple_of((h * NODES + at) * LANES, LANES)
             table[pl.ds(begin, LANES)] = jnp.concatenate(parts).T
         table_copy(h, s).start()
+        rim_sums(h, s, four_rows(ids_ref[tile, pl.ds(h * LANES, LANES)], s))
+
+    def lists_part(first, last):
+        def go(i, _):
+            lists_block(i, ids_ref, lists_state)
+            return 0
+        lax.fori_loop(first, last, go, 0)
 
     stage_copy(0).start()
     stage_copy(1).start()
     barrier = pltpu.get_barrier_semaphore()
     each(lambda t: pl.semaphore_signal(barrier, inc=1, device_id={"four": (me + t) % GROUP}, device_id_type=MESH))
+    for off in (1, N_MESH - 1):
+        pl.semaphore_signal(
+            barrier, inc=1, device_id={"mesh": (lax.axis_index("mesh") + off) % N_MESH}, device_id_type=MESH
+        )
     turn(0)
-    pl.semaphore_wait(barrier, GROUP - 1)
+    pl.semaphore_wait(barrier, GROUP + 1)
     send_rows(0)
     differentiate(0)
     send_slopes(0)
@@ -289,13 +336,23 @@
         if f + 2 < 12:
             stage_copy(f + 2).start()
 
+    for g in range(4):
+        own = four_rows(geometry_ref[g, pl.ds(pair(me), 8), :], me)
+        for n in range(4):
+            geo[g, n] = own[n : n + 1]
+
     relays(0)
     send_rows(1)
     send_slopes(1)
+    lists_start(lists_state)
+    rim_start()
+    lists_part(0, 4)
     compute(0)
     own_back(0).start()
     relays(1)
     each(lambda t: back_copy(0, t).start())
+    lists_part(4, 8)
+    lists_end(rim_ref, lists_state, place_ref, rep_ref, rim_at_ref)
     compute(1)
     own_back(1).start()
     each(lambda t: back_copy(1, t).start())
@@ -310,6 +367,13 @@
             finish(h, src)
             return 0
         lax.fori_loop(1, GROUP, arrive, 0)
+
+    for side in range(2):
+        rim_copy(side).start()
+    for side in range(2):
+        rim_copy(side).wait_recv()
+        rim_copy(side).wait_send()
+    rims_ref[...] = rims[...] + met[...]
 
     for h in range(HALVES):
         for dx, k in SENT:
@@ -326,7 +390,7 @@
         lax.fori_loop(0, GROUP, drained, 0)
 
 
-def step(u, base, geo, mass):
+def step(u, base, geometry, mass, ids, rim):
     synth, anal = plane_tables()
     vmem = pl.BlockSpec(memory_space=pltpu.VMEM)
     hbm = pl.BlockSpec(memory_space=pl.ANY)
@@ -334,9 +398,15 @@
     dma = pltpu.SemaphoreType.DMA
     return pl.pallas_call(
         step_kernel,
-        out_shape=jax.ShapeDtypeStruct((POINTS, 128), f32),
-        in_specs=[vmem, hbm, vmem, vmem, vmem, vmem],
-        out_specs=hbm,
+        out_shape=(
+            jax.ShapeDtypeStruct((POINTS, 128), f32),
+            jax.ShapeDtypeStruct((LIST_ROWS, 128), jnp.int32),
+            jax.ShapeDtypeStruct((LIST_ROWS, 128), jnp.int32),
+            jax.ShapeDtypeStruct((2, RIM_PAD), jnp.int32),
+            jax.ShapeDtypeStruct((2 * RIM_PAD, 128), f32),
+        ),
+        in_specs=[vmem, hbm] + [vmem] * 6,
+        out_specs=(hbm, vmem, vmem, vmem, vmem),
         scratch_shapes=[
             pltpu.VMEM((HALVES, 3, NODES, COEFS, LANES), f32),
             pltpu.VMEM((HALVES, 3, NODES, COEFS, LANES), f32),
@@ -353,15 +423,30 @@
             dma((HALVES, 8)), dma((HALVES, 8)), dma((HALVES, GROUP)), dma((HALVES, GROUP)),
             dma((HALVES, GROUP)), dma((HALVES, GROUP)), dma((HALVES, GROUP)),
             dma((HALVES, 3)), dma((2,)), dma((HALVES, GROUP)),
+            pltpu.VMEM((4, 4, 1, E_DEV), f32),
+            pltpu.VMEM((2 * RIM_PAD, 128), f32),
+            pltpu.VMEM((2 * RIM_PAD, 128), f32),
+            pltpu.VMEM((2 * RIM_PAD, 128), f32),
+            dma((2,)), dma((2,)),
+            pltpu.VMEM((128, 128), f32),
+            pltpu.VMEM((256, 128), f32),
+            pltpu.VMEM((512, 128), f32),
+            pltpu.VMEM((8, 128), f32),
         ],
         compiler_params=pltpu.CompilerParams(
             collective_id=0, has_side_effects=True, vmem_limit_bytes=VMEM_LIMIT
         ),
         name="step",
-    )(u, base, geo, mass, jnp.asarray(synth), jnp.asarray(anal))
-
-
-def lists_block(n, ids_ref, state):
+    )(u, base, geometry, mass, ids, rim, jnp.asarray(synth), jnp.asarray(anal))
+
+
+def lists_block(i, ids_ref, state):
+    tile = ids_ref[pl.ds(pl.multiple_of(i * 8, 8), 8), :]
+    for j in range(8):
+        lists_row(i * 8 + j, tile[j : j + 1], state)
+
+
+def lists_row(n, ids, state):
     counts, firsts, lists, used = state
     bf, f32 = jnp.bfloat16, jnp.float32
     width = E_DEV
@@ -372,34 +457,35 @@
     def flat(left, right):
         return lax.dot_general(left, right, (((1,), (1,)), ((), ())), preferred_element_type=f32)
 
-    ids = ids_ref[n]
     digit = iota((128, width), 0)
     high = (digit == ids // 128).astype(bf)
     low = (digit == ids % 128).astype(bf)
-    prior = jnp.sum(low.astype(f32) * jnp.dot(counts[...].astype(bf), high, preferred_element_type=f32), axis=0, keepdims=True)
+    low_f = low.astype(f32)
+    earlier = iota((width, width), 0) < iota((width, width), 1)
+    prior = jnp.sum(low_f * jnp.dot(counts[...].astype(bf), high, preferred_element_type=f32), axis=0, keepdims=True)
     across = jnp.broadcast_to(ids.astype(f32), (width, width))
-    same = jnp.where((across == across.T) & (iota((width, width), 0) < iota((width, width), 1)), 1.0, 0.0)
-    again = jnp.where(prior + jnp.sum(same, axis=0, keepdims=True) > 0, 1.0, 0.0)
+    same = jnp.where((across == across.T) & earlier, 1.0, 0.0)
+    prior = prior + jnp.sum(same, axis=0, keepdims=True)
     counts[...] = counts[...] + flat(low, high)
     lane = iota((1, width), 1)
     block = ((lane // LANES) * NODES + n).astype(f32)
     inner = (lane % LANES).astype(f32)
-    once = 1.0 - again
-    low_f = low.astype(f32)
+    once = jnp.where(prior == 0, 1.0, 0.0)
     firsts[...] = firsts[...] + flat(
         jnp.concatenate([low_f * (once * block), low_f * (once * inner)]).astype(bf), high
     )
     found = jnp.dot(firsts[...].astype(bf), high, preferred_element_type=f32)
     rep_block = jnp.sum(found[0:128] * low_f, axis=0, keepdims=True)
     rep_inner = jnp.sum(found[128:256] * low_f, axis=0, keepdims=True)
+    second = jnp.where(prior == 1, 1.0, 0.0)
+    further = jnp.where(prior > 1, 1.0, 0.0)
+    kinds = jnp.concatenate([second, further, jnp.zeros((6, width), f32)])
     before = jnp.dot(
-        jnp.broadcast_to(again, (8, width)).astype(bf),
-        jnp.where(iota((width, width), 0) < iota((width, width), 1), 1.0, 0.0).astype(bf),
-        preferred_element_type=f32,
-    )[0:1]
-    slot = (before + used[0:1, 0:1]).astype(jnp.int32)
-    used[...] = used[...] + jnp.sum(again, axis=1, keepdims=True)
-    slot_low = jnp.where(digit == slot % 128, again, 0.0)
+        kinds.astype(bf), jnp.where(earlier, 1.0, 0.0).astype(bf), preferred_element_type=f32
+    ) + used[:, 0:1]
+    used[...] = used[...] + jnp.sum(kinds, axis=1, keepdims=True)
+    slot = jnp.where(second > 0, before[0:1], LISTED - 1 - before[1:2]).astype(jnp.int32)
+    slot_low = jnp.where(digit == slot % 128, second + further, 0.0)
     slot_high = (digit == slot // 128).astype(bf)
     left = jnp.concatenate([slot_low * v for v in (block, inner, rep_block, rep_inner)]).astype(bf)
     lists[...] = lists[...] + flat(left, slot_high)
@@ -414,154 +500,115 @@
     counts, firsts, lists, used = state
     bf, f32 = jnp.bfloat16, jnp.float32
     index = lax.broadcasted_iota(jnp.int32, (128, 128), 0) * 128 + lax.broadcasted_iota(jnp.int32, (128, 128), 1)
+    front = used[0:1, 0:1].astype(jnp.int32)
+    end = LISTED - used[1:2, 0:1].astype(jnp.int32)
     for k, ref in enumerate((place_ref, rep_ref)):
         at = lists[256 * k : 256 * k + 128] * 128.0 + lists[256 * k + 128 : 256 * k + 256]
-        ref[...] = jnp.where(index < EXTRA, at.T.astype(jnp.int32), POINTS)[0:LIST_ROWS]
-    rim = rim_ref[...]
-    digit = lax.broadcasted_iota(jnp.int32, (128, RIM_PAD), 0)
-    high = (digit == rim // 128).astype(bf)
-    low = (digit == rim % 128).astype(f32)
-    found = jnp.dot(firsts[...].astype(bf), high, preferred_element_type=f32)
-    rep_block = jnp.sum(found[0:128] * low, axis=0, keepdims=True)
-    rep_inner = jnp.sum(found[128:256] * low, axis=0, keepdims=True)
-    rim_at_ref[...] = (rep_block * 128.0 + rep_inner).astype(jnp.int32)
-
-
-def lists_kernel(ids_ref, rim_ref, place_ref, rep_ref, rim_at_ref, *state):
-    lists_start(state)
-
-    def go(n, _):
-        lists_block(n, ids_ref, state)
+        filled = (index < front) | (index >= end)
+        entries = jnp.where(filled, at.T.astype(jnp.int32), POINTS)
+        ref[...] = jnp.where(index < LISTED, entries, front)[0:LIST_ROWS]
+    rim = rim_ref[0]
+    rim_at_ref[...] = jnp.zeros_like(rim_at_ref)
+    digit = lax.broadcasted_iota(jnp.int32, (128, RIM), 0)
+    for k in range(2):
+        ids = rim[k : k + 1]
+        high = (digit == ids // 128).astype(bf)
+        low = (digit == ids % 128).astype(f32)
+        found = jnp.dot(firsts[...].astype(bf), high, preferred_element_type=f32)
+        rep_block = jnp.sum(found[0:128] * low, axis=0, keepdims=True)
+        rep_inner = jnp.sum(found[128:256] * low, axis=0, keepdims=True)
+        rim_at_ref[k : k + 1, 0:RIM] = (rep_block * 128.0 + rep_inner).astype(jnp.int32)
+
+
+def assemble_kernel(place_ref, rep_ref, rim_ref, table_ref, rims_ref, out_ref, table, out, sem, out_sem):
+    load = pltpu.make_async_copy(table_ref, table.at[pl.ds(0, POINTS)], sem.at[0])
+    load.start()
+    table[pl.ds(POINTS, 8)] = jnp.zeros((8, 1, 128), jnp.float32)
+    load.wait()
+    front = place_ref[LIST_ROWS * 128 - 1]
+
+    def add(t, _):
+        at = [rep_ref[t * BATCH + k] for k in range(BATCH)]
+        vals = [table[at[k]] + table[place_ref[t * BATCH + k]] for k in range(BATCH)]
+        for k in range(BATCH):
+            table[at[k]] = vals[k]
         return 0
-    lax.fori_loop(0, NODES, go, 0)
-    lists_end(rim_ref, state, place_ref, rep_ref, rim_at_ref)
-
-
-LIST_STATE = [
-    pltpu.VMEM((128, 128), jnp.float32),
-    pltpu.VMEM((256, 128), jnp.float32),
-    pltpu.VMEM((512, 128), jnp.float32),
-    pltpu.VMEM((8, 128), jnp.float32),
-]
-LIST_SHAPES = (
-    jax.ShapeDtypeStruct((LIST_ROWS, 128), jnp.int32),
-    jax.ShapeDtypeStruct((LIST_ROWS, 128), jnp.int32),
-    jax.ShapeDtypeStruct((1, RIM_PAD), jnp.int32),
-)
-
-
-def node_lists(connect, edges):
-    vmem = pl.BlockSpec(memory_space=pltpu.VMEM)
-    rim = jnp.pad(edges.reshape(1, -1), ((0, 0), (0, RIM_PAD - 2 * RIM)))
-    return pl.pallas_call(
-        lists_kernel,
-        out_shape=LIST_SHAPES,
-        in_specs=[vmem] * 2,
-        out_specs=(vmem,) * 3,
-        scratch_shapes=LIST_STATE,
-        compiler_params=pltpu.CompilerParams(vmem_limit_bytes=VMEM_LIMIT),
-        name="lists",
-    )(connect.reshape(NODES, 1, E_DEV), rim)
-
-
-def gather_kernel(place_ref, rep_ref, rim_ref, table_ref, summed_ref, rims_ref, table, sems):
-    load = pltpu.make_async_copy(table_ref, table.at[pl.ds(0, POINTS)], sems.at[0])
-    load.start()
-    table[pl.ds(POINTS, 8)] = jnp.zeros((8, 128), jnp.float32)
-    load.wait()
-
-    def add(t, _):
-        for k in range(8):
-            at = pl.ds(rep_ref[t // 16, (t % 16) * 8 + k], 1)
-            table[at] = table[at] + table[pl.ds(place_ref[t // 16, (t % 16) * 8 + k], 1)]
+    lax.fori_loop(0, (front + BATCH - 1) // BATCH, add, 0)
+
+    def add_further(t, _):
+        at = rep_ref[LISTED - 1 - t]
+        table[at] = table[at] + table[place_ref[LISTED - 1 - t]]
         return 0
-    lax.fori_loop(0, (EXTRA + 7) // 8, add, 0)
-    store = pltpu.make_async_copy(table.at[pl.ds(0, POINTS)], summed_ref, sems.at[0])
-    store.start()
-
-    def pick(t, _):
-        for k in range(9):
-            rims_ref[pl.ds(t * 9 + k, 1)] = table[pl.ds(rim_ref[0, t * 9 + k], 1)]
+    lax.fori_loop(0, EXTRA - front, add_further, 0)
+
+    def meet(t, _):
+        for side in range(2):
+            for k in range(9):
+                table[rim_ref[side * RIM_PAD + t * 9 + k]] = rims_ref[side * RIM_PAD + t * 9 + k]
         return 0
-    lax.fori_loop(0, 2 * RIM // 9, pick, 0)
-    store.wait()
-
-
-def spread_kernel(place_ref, rep_ref, rim_ref, summed_ref, lower_ref, upper_ref, out_ref, table, sems):
-    load = pltpu.make_async_copy(summed_ref, table.at[pl.ds(0, POINTS)], sems.at[0])
-    load.start()
-    table[pl.ds(POINTS, 8)] = jnp.zeros((8, 128), jnp.float32)
-    load.wait()
-
-    def add(t, _):
-        for k in range(9):
-            at = pl.ds(rim_ref[0, t * 9 + k], 1)
-            table[at] = table[at] + lower_ref[pl.ds(t * 9 + k, 1)]
-        for k in range(9):
-            at = pl.ds(rim_ref[0, RIM + t * 9 + k], 1)
-            table[at] = table[at] + upper_ref[pl.ds(t * 9 + k, 1)]
+    lax.fori_loop(0, RIM // 9, meet, 0)
+
+    def spread(t, _):
+        vals = [table[rep_ref[t * BATCH + k]] for k in range(BATCH)]
+        for k in range(BATCH):
+            table[place_ref[t * BATCH + k]] = vals[k]
         return 0
-    lax.fori_loop(0, RIM // 9, add, 0)
-
-    def spread(t, _):
-        vals = [table[pl.ds(rep_ref[t // 16, (t % 16) * 8 + k], 1)] for k in range(8)]
-        for k in range(8):
-            table[pl.ds(place_ref[t // 16, (t % 16) * 8 + k], 1)] = vals[k]
-        return 0
-    lax.fori_loop(0, (EXTRA + 7) // 8, spread, 0)
+    lax.fori_loop(0, LISTED // BATCH, spread, 0)
+
+    def block_copy(t):
+        at = (
+            slice(None),
+            pl.ds(pl.multiple_of((t % 8) * 8, 8), 8),
+            pl.ds(pl.multiple_of((t // 8) * LANES, LANES), LANES),
+        )
+        return pltpu.make_async_copy(out.at[at], out_ref.at[at], out_sem.at[t])
 
     def write(t, _):
         h, i = t // 8, t % 8
         parts = []
         for j in range(8):
             begin = pl.multiple_of((h * NODES + i * 8 + j) * LANES, LANES)
-            cols = table[pl.ds(begin, LANES)].T
+            cols = table[pl.ds(begin, LANES)].reshape(LANES, 128).T
             parts.append(cols[0:48] / cols[48:49])
         block = jnp.swapaxes(jnp.stack(parts), 0, 1)
-        out_ref[:, pl.ds(pl.multiple_of(i * 8, 8), 8), pl.ds(pl.multiple_of(h * LANES, LANES), LANES)] = block
+        out[:, pl.ds(pl.multiple_of(i * 8, 8), 8), pl.ds(pl.multiple_of(h * LANES, LANES), LANES)] = block
+        block_copy(t).start()
         return 0
     lax.fori_loop(0, 16, write, 0)
 
-
-def assemble(table, connect, edges):
-    place, rep, rim_at = node_lists(connect, edges)
+    def written(t, _):
+        block_copy(t).wait()
+        return 0
+    lax.fori_loop(0, 16, written, 0)
+
+
+def assemble(table, place, rep, rim_at, rims):
     smem = pl.BlockSpec(memory_space=pltpu.SMEM)
     vmem = pl.BlockSpec(memory_space=pltpu.VMEM)
     hbm = pl.BlockSpec(memory_space=pl.ANY)
     f32 = jnp.float32
-    params = pltpu.CompilerParams(vmem_limit_bytes=VMEM_LIMIT)
-    scratch = [pltpu.VMEM((POINTS + 8, 128), f32), pltpu.SemaphoreType.DMA((1,))]
-    summed, rims = pl.pallas_call(
-        gather_kernel,
-        out_shape=(jax.ShapeDtypeStruct((POINTS, 128), f32), jax.ShapeDtypeStruct((2 * RIM, 128), f32)),
-        in_specs=[smem, smem, smem, hbm],
-        out_specs=(hbm, vmem),
-        scratch_shapes=scratch,
-        compiler_params=params,
-        name="gather",
-    )(place, rep, rim_at, table.reshape(POINTS, 128))
-    count = lax.axis_size("mesh")
-    up = [(i, (i + 1) % count) for i in range(count)]
-    down = [(j, i) for i, j in up]
-    from_lower = lax.ppermute(rims[RIM:], "mesh", up)
-    from_upper = lax.ppermute(rims[:RIM], "mesh", down)
     return pl.pallas_call(
-        spread_kernel,
+        assemble_kernel,
         out_shape=jax.ShapeDtypeStruct((3 * COEFS, NODES, E_DEV), f32),
-        in_specs=[smem, smem, smem, hbm, vmem, vmem],
-        out_specs=vmem,
-        scratch_shapes=scratch,
-        compiler_params=params,
-        name="spread",
-    )(place, rep, rim_at, summed, from_lower, from_upper)
+        in_specs=[smem, smem, smem, hbm, vmem],
+        out_specs=hbm,
+        scratch_shapes=[
+            pltpu.VMEM((POINTS + 8, 1, 128), f32),
+            pltpu.VMEM((3 * COEFS, NODES, E_DEV), f32),
+            pltpu.SemaphoreType.DMA((1,)),
+            pltpu.SemaphoreType.DMA((16,)),
+        ],
+        compiler_params=pltpu.CompilerParams(vmem_limit_bytes=VMEM_LIMIT),
+        name="assemble",
+    )(
+        place.reshape(-1), rep.reshape(-1), rim_at.reshape(-1),
+        table.reshape(POINTS, 1, 128), rims.reshape(2 * RIM_PAD, 1, 128),
+    )
 
 
 def body(adj_modes, base_flow, geometry, mass, connect, edge_nodes):
-    me = lax.axis_index("four")
-    geo = lax.dynamic_slice_in_dim(geometry, me * 4, 4, 1).reshape(4, 4, 1, E_DEV)
-    table = step(adj_modes, base_flow, geo, mass.reshape(NODES, 1, E_DEV))
-    out = assemble(table, connect, edge_nodes[0])
-    return out.reshape(adj_modes.shape)
+    table, *lists = step(adj_modes, base_flow, geometry, mass, connect, edge_nodes)
+    return assemble(table, *lists).reshape(adj_modes.shape)
 
 
 def solution(mesh):

time: 377 us -> 295 us (0.78)
  Pallas kernels: 357 us -> 293 us
  waiting for transfers between devices: 7.87 us -> 0 us
  local copies, waits for them, and re-layouts: 6.65 us -> 1.25 us
  starting transfers between devices: 4.03 us -> 0 us
    pallas_call x4 -> x2, Pallas kernels: 357 us -> 293 us  [the longest x1 265 us: step(): pl.pallas_call(step_kernel, out_shape=(jax.ShapeDtypeStruct((POINTS, 128)...]
    ppermute x2 -> x0, waiting for transfers between devices: 7.87 us -> none  [the longest x1 5.47 us: assemble(): from_lower = lax.ppermute(rims[RIM:], 'mesh', up)]
    ppermute x2 -> x0, starting transfers between devices: 4.03 us -> none  [the longest x1 4.03 us: assemble(): from_upper = lax.ppermute(rims[:RIM], 'mesh', down)]
  transfers between devices with their start and end apart: 2 -> 0, of which waited for: 2 -> 0; matrix products, arithmetic and copies ran while one was open for 0% -> 0% of each run, Pallas kernels for 0% -> 0%
where the time goes in v2:
time: 295 us; the launch traced here: 294 us
  Pallas kernels  293 us (99%)
    pallas_call x1, Pallas kernels, step(): pl.pallas_call(step_kernel, out_shape=(jax.ShapeDtypeStruct((POINTS, 128)...  265 us
    pallas_call x1, Pallas kernels, assemble(): pl.pallas_call(assemble_kernel, out_shape=jax.ShapeDtypeStruct((3 * COEFS...  27.7 us

profile of v2, /device:TPU:2, one launch (start us, length us, event | category | flops | bytes accessed | tf_op | source)
XLA Modules:
  0.0 294.3 jit_solution(2222117030474526931)
XLA Ops:
  0.0 265.4 %step.1 = (f32[16384,128]{1,0:T(8,128)}, s32[32,128]{1,0:T(8,128)}, s32[32,128]{1,0:T(8,128)}, s32[2,256]{1,0:T(2,128)}, f32[512,128]{1,0:T(8,128)}) custom-call(f32[3,16,64,256]{3,2,1,0:T(8,128)} %u_ref.1, bf16[12,256,4,256]{3,2,1,0:T(4,128)(2,1)} %base_ref.1, f32[4,64,256]{2,1,0:T(8,128)} %geometry_ref.1, f32[64,256]{1,0:T(8,128)} %mass_ref.1, ...), custom_call_target="tpu_custom_call" | custom-call | tf_op jit(solution)/shard_map/step/pallas_call | solution.py:399
  265.4 1.2 copy.9
  266.6 27.7 %assemble.1 = f32[48,64,256]{2,1,0:T(8,128)} custom-call(s32[4096]{0:T(1024)} %bitcast.9, s32[4096]{0:T(1024)} %bitcast.10, s32[512]{0:T(512)} %bitcast.11, f32[16384,1,128]{2,1,0:T(1,128)} %bitcast.7, f32[512,1,128]{2,1,0:T(1,128)} %bitcast.8), custom_call_target="tpu_custom_call" | custom-call | tf_op jit(solution)/shard_map/assemble/pallas_call | solution.py:590

commit v3 on v2

v3 whole, which is shorter than its diff:
```python
import functools
import math

import jax
import jax.numpy as jnp
import numpy as np
from jax import lax
from jax.experimental import pallas as pl
from jax.experimental.pallas import tpu as pltpu
from jax.sharding import PartitionSpec as P

NP = 8
NODES = 64
PLANES = 256
UNIQUE = 12825
E_DEV = 256
POINTS = NODES * E_DEV
EXTRA = POINTS - UNIQUE
BATCH = 8
LISTED = (EXTRA + BATCH + 127) // 128 * 128
LIST_ROWS = (LISTED // 128 + 8) // 8 * 8
PLACES = LIST_ROWS * 128
RIM = 225
RIM_PAD = 256
HALVES = 2
LANES = E_DEV // HALVES
N_MESH = 16
GROUP = 16
COEFS = PLANES // GROUP
STEP_SIZE = 0.1
HIGH = lax.Precision.HIGHEST
MESH = pl.DeviceIdType.MESH
VMEM_LIMIT = 60 * 2**20


def legendre_values(degree, point):
    before = 1.0
    current = point
    for order in range(1, degree):
        after = ((2 * order + 1) * point * current - order * before) / (order + 1)
        before = current
        current = after
    return (current, before)


def gll_derivative(points_n):
    degree = points_n - 1
    points = []
    for index in range(points_n):
        point = -math.cos(math.pi * index / degree)
        for sweep in range(100):
            top_val, below_val = legendre_values(degree, point)
            point = point - (point * top_val - below_val) / (points_n * top_val)
        points.append(point)
    values = [legendre_values(degree, point)[0] for point in points]
    rows = [
        [
            0.0 if r == c else values[r] / (values[c] * (points[r] - points[c]))
            for c in range(points_n)
        ]
        for r in range(points_n)
    ]
    rows[0][0] = -degree * (degree + 1) / 4.0
    rows[degree][degree] = degree * (degree + 1) / 4.0
    return np.asarray(rows, np.float32)


def plane_tables():
    plane = np.arange(PLANES)
    wave = plane // 2
    phase = (plane[:, None] * wave[None, :] % PLANES) * (2.0 * math.pi / PLANES)
    synth = np.where(plane[None, :] % 2 == 1, np.sin(phase), np.cos(phase))
    synth[:, 1] = 1 - 2 * (plane % 2)
    scales = np.where(wave == 0, 1.0 / PLANES, 2.0 / PLANES)
    analysis = synth.T * scales[:, None]
    number = wave * (2.0 / PLANES)
    axial = np.zeros((PLANES, PLANES))
    axial[plane[::2], plane[1::2]] = number[::2]
    axial[plane[1::2], plane[::2]] = -number[1::2]
    both = np.concatenate([synth, synth @ axial])
    return both.astype(np.float32), (STEP_SIZE * analysis).astype(np.float32)


def step_kernel(
    u_ref, base_ref, geometry_ref, mass_ref, ids_ref, rim_ref, synth_ref, anal_ref,
    table_ref, lists_ref, rims_ref,
    u, ut, along, rows, slopes, base, stage, inputs, fields, forcing, back, returned, table,
    row_send, relay_send, slope_send, back_send, row_recv, slope_recv, back_recv,
    own_sem, stage_sem, table_sem, u_sem, geo, rim_ids, rim_parts, rims, met, rim_send, rim_recv, *lists_state,
):
    deriv = gll_derivative(NP)
    me = lax.axis_index("four")
    x, z = me // 8, me % 8
    odd = z % 2
    sign = 1 - 2 * odd
    partner = x * 8 + z + sign

    def remote(src, dst, send, recv, to):
        return pltpu.make_async_remote_copy(
            src_ref=src, dst_ref=dst, send_sem=send, recv_sem=recv,
            device_id={"four": to}, device_id_type=MESH,
        )

    def source(dx, k):
        return ((x + dx) % 2) * 8 + (z - sign * k + 8) % 8

    def target(dx, k):
        off = (0, 2, -1, -3)[k]
        return ((x + dx) % 2) * 8 + (z + sign * off + 8) % 8

    def pair(dev):
        return pl.multiple_of((dev // 2) * 8, 8)

    def stage_copy(f):
        return pltpu.make_async_copy(base_ref.at[f], stage.at[f % 2], stage_sem.at[f % 2])

    def u_copy(h):
        return pltpu.make_async_copy(u_ref.at[:, :, :, pl.ds(h * LANES, LANES)], u.at[h], u_sem.at[h])

    def turn(h):
        u_copy(h).wait()
        def block(t, _):
            c = t // 8
            i = pl.multiple_of((t % 8) * 8, 8)
            ut[h, c, pl.ds(i, 8)] = jnp.swapaxes(u[h, c, :, pl.ds(i, 8)], 0, 1)
            return 0
        lax.fori_loop(0, 24, block, 0)

    def differentiate(h):
        def block(t, _):
            c, j = t // 8, t % 8
            vals = [ut[h, c, 8 * i + j] for i in range(8)]
            for i in range(8):
                total = vals[0] * float(deriv[i, 0])
                for k in range(1, 8):
                    total = total + vals[k] * float(deriv[i, k])
                along[h, c, 8 * i + j] = total
            return 0
        lax.fori_loop(0, 24, block, 0)

    def u_rows(h, dev):
        return u_ref.at[:, :, pl.ds(pair(dev), 8), pl.ds(h * LANES, LANES)]

    def row_copy(h, dx, k):
        to = target(dx, k)
        return remote(u_rows(h, to), rows.at[h, me], row_send.at[h, dx * 4 + k], row_recv.at[h, me], to)

    def own_relay(h):
        return remote(u_rows(h, me), rows.at[h, me], relay_send.at[h, 0], row_recv.at[h, me], partner)

    def relay(h, dx, k):
        src = source(dx, k)
        return remote(rows.at[h, src], rows.at[h, src], relay_send.at[h, dx * 4 + k], row_recv.at[h, src], partner)

    def far_source(dx, k):
        return ((x + dx) % 2) * 8 + (z + sign + sign * k + 8) % 8

    def row_wait(h, src):
        remote(rows.at[h, src], rows.at[h, src], relay_send.at[h, 0], row_recv.at[h, src], partner).wait_recv()

    def slope_copy(h, t):
        to = (me + t) % GROUP
        return remote(
            along.at[h, :, pl.ds(to * 4, 4)], slopes.at[h, me], slope_send.at[h, t], slope_recv.at[h, me], to
        )

    def slope_wait(h, t):
        src = (me + t) % GROUP
        remote(slopes.at[h, src], slopes.at[h, src], slope_send.at[h, t], slope_recv.at[h, src], src).wait_recv()

    def back_copy(h, g, t):
        to = (me + t) % GROUP
        return remote(
            back.at[h, g, to], returned.at[h, g, me], back_send.at[h, g, t], back_recv.at[h, g, me], to
        )

    def back_wait(h, g, src):
        remote(
            returned.at[h, g, src], returned.at[h, g, src], back_send.at[h, g, 0], back_recv.at[h, g, src], partner
        ).wait_recv()

    def own_copies(h):
        return (
            pltpu.make_async_copy(u_rows(h, me), rows.at[h, me], own_sem.at[h, 0]),
            pltpu.make_async_copy(along.at[h, :, pl.ds(me * 4, 4)], slopes.at[h, me], own_sem.at[h, 1]),
        )

    def own_back(h, g):
        return pltpu.make_async_copy(back.at[h, g, me], returned.at[h, g, me], own_sem.at[h, 2 + g])

    def send_back(h, g):
        own_back(h, g).start()
        each(lambda t: back_copy(h, g, t).start())

    NEAR = [(1, 0), (0, 1), (1, 1), (0, 2), (1, 2), (0, 3), (1, 3)]
    SENT = [(0, 3), (1, 3), (0, 1), (1, 1), (0, 2), (1, 2), (1, 0)]

    def each(fn):
        def go(t, _):
            fn(t)
            return 0
        lax.fori_loop(1, GROUP, go, 0)

    def send_rows(h):
        for dx, k in SENT:
            row_copy(h, dx, k).start()
        own_relay(h).start()

    def send_slopes(h):
        each(lambda t: slope_copy(h, t).start())

    def relays(h):
        for dx, k in NEAR:
            row_wait(h, source(dx, k))
            relay(h, dx, k).start()

    def compute(h, after):
        for copy in own_copies(h):
            copy.wait()
        for k in range(4):
            for dx in range(2):
                row_wait(h, far_source(dx, k))
        each(lambda t: slope_wait(h, t))

        def gather(s, _):
            at = pl.ds(pl.multiple_of(s * COEFS, COEFS), COEFS)
            for c in range(3):
                turned = jnp.swapaxes(rows[h, s, c], 0, 1)
                line = [turned[j] for j in range(8)]
                for n in range(4):
                    total = None
                    for k in range(8):
                        term = line[k] * jnp.where(odd == 1, float(deriv[4 + n, k]), float(deriv[n, k]))
                        total = term if total is None else total + term
                    inputs[n, at, pl.ds(c * LANES, LANES)] = jnp.where(odd == 1, line[4 + n], line[n])
                    inputs[n, at, pl.ds((3 + c) * LANES, LANES)] = total
                    inputs[n, at, pl.ds((6 + c) * LANES, LANES)] = slopes[h, s, c, n]
            return 0
        lax.fori_loop(0, GROUP, gather, 0)

        def node(n, _):
            fields[:, 0 : 9 * LANES] = jnp.dot(
                synth_ref[0:PLANES], inputs[n], precision=HIGH, preferred_element_type=jnp.float32
            )
            fields[:, 9 * LANES : 12 * LANES] = jnp.dot(
                synth_ref[PLANES : 2 * PLANES], inputs[n, :, 0 : 3 * LANES],
                precision=HIGH, preferred_element_type=jnp.float32,
            )
            metric = [geo[g, n, :, pl.ds(h * LANES, LANES)] for g in range(4)]

            def planes(p, _):
                at = pl.ds(pl.multiple_of(p * 16, 16), 16)
                flow = [base[f, n, at, pl.ds(h * LANES, LANES)].astype(jnp.float32) for f in range(12)]
                get = lambda f: fields[at, f * LANES : (f + 1) * LANES]
                on_r = flow[0] * metric[0] + flow[1] * metric[2]
                on_s = flow[0] * metric[1] + flow[1] * metric[3]
                vel = [get(c) for c in range(3)]
                for c in range(3):
                    total = vel[0] * flow[3 + 3 * c] + vel[1] * flow[4 + 3 * c] + vel[2] * flow[5 + 3 * c]
                    total = total - on_r * get(6 + c) - on_s * get(3 + c) - flow[2] * get(9 + c)
                    forcing[at, c * LANES : (c + 1) * LANES] = total
                return 0
            lax.fori_loop(0, PLANES // 16, planes, 0)
            modes = jnp.dot(anal_ref[...], forcing[...], precision=HIGH, preferred_element_type=jnp.float32)
            for c in range(3):
                back[h, n // 2, :, n % 2, c] = modes[:, c * LANES : (c + 1) * LANES].reshape(GROUP, COEFS, LANES)
            return 0
        for g in range(2):
            lax.fori_loop(2 * g, 2 * g + 2, node, 0)
            after(g)

    def table_copy(h, g, s):
        at = pl.ds(pl.multiple_of((h * NODES + 4 * s + 2 * g) * LANES, 2 * LANES), 2 * LANES)
        return pltpu.make_async_copy(table.at[at], table_ref.at[at], table_sem.at[h, g, s])

    def four_rows(block, s):
        return jnp.where(s % 2 == 1, block[4:8], block[0:4])

    def rim_start():
        for k in range(2):
            row = jnp.concatenate([rim_ref[0, k : k + 1], jnp.full((1, RIM_PAD - RIM), -1, jnp.int32)], axis=1)
            rim_ids[k * RIM_PAD : (k + 1) * RIM_PAD] = jnp.broadcast_to(row.astype(jnp.float32), (128, RIM_PAD)).T
        rim_parts[...] = jnp.zeros_like(rim_parts)

    def rim_sums(values, ids):
        pieces = []
        for _ in range(3):
            pieces.append(values.astype(jnp.bfloat16))
            values = values - pieces[-1].astype(jnp.float32)
        hit = jnp.concatenate([(rim_ids[...] == row.astype(jnp.float32)).astype(jnp.bfloat16) for row in ids], axis=1)
        rim_parts[...] = rim_parts[...] + lax.dot_general(
            hit, jnp.concatenate(pieces), (((1,), (1,)), ((), ())), preferred_element_type=jnp.float32
        )

    def rim_total():
        parts = rim_parts[...]
        total = parts[:, 0:64] + (parts[:, 64:128] + parts[:, 128:192])
        rims[...] = jnp.concatenate([total, jnp.zeros_like(total)], axis=1)

    def rim_copy(side):
        to = (lax.axis_index("mesh") + (N_MESH - 1 if side == 0 else 1)) % N_MESH
        return pltpu.make_async_remote_copy(
            src_ref=rims.at[pl.ds(side * RIM_PAD, RIM_PAD)], dst_ref=met.at[pl.ds((1 - side) * RIM_PAD, RIM_PAD)],
            send_sem=rim_send.at[side], recv_sem=rim_recv.at[1 - side],
            device_id={"mesh": to}, device_id_type=MESH,
        )

    def finish(h, g, s):
        tile = pl.ds(pl.multiple_of((s // 2) * 8, 8), 8)
        half = pl.ds(h * LANES, LANES)
        weights = four_rows(mass_ref[tile, half], s)
        ids = four_rows(ids_ref[tile, half], s)
        tall = []
        for n in range(2):
            at = 4 * s + 2 * g + n
            weight = weights[2 * g + n : 2 * g + n + 1]
            parts = [(ut[h, c, at] + returned[h, g, s, n, c]) * weight for c in range(3)]
            parts.append(jnp.broadcast_to(weight, (8, LANES)))
            parts.append(jnp.zeros((8, LANES), jnp.float32))
            tall.append(jnp.concatenate(parts))
            begin = pl.multiple_of((h * NODES + at) * LANES, LANES)
            table[pl.ds(begin, LANES)] = jnp.concatenate([tall[-1], jnp.zeros((64, LANES), jnp.float32)]).T
        table_copy(h, g, s).start()
        rim_sums(jnp.concatenate(tall, axis=1), [ids[2 * g + n : 2 * g + n + 1] for n in range(2)])

    def lists_part(block):
        def go(i, _):
            block(i, ids_ref, lists_state)
            return 0
        lax.fori_loop(0, NODES // 8, go, 0)

    for h in range(HALVES):
        u_copy(h).start()
    barrier = pltpu.get_barrier_semaphore()
    each(lambda t: pl.semaphore_signal(barrier, inc=1, device_id={"four": (me + t) % GROUP}, device_id_type=MESH))
    for off in (1, N_MESH - 1):
        pl.semaphore_signal(
            barrier, inc=1, device_id={"mesh": (lax.axis_index("mesh") + off) % N_MESH}, device_id_type=MESH
        )
    pl.semaphore_wait(barrier, GROUP + 1)
    send_rows(0)
    turn(0)
    differentiate(0)
    send_slopes(0)
    for copy in own_copies(0):
        copy.start()
    stage_copy(0).start()
    stage_copy(1).start()
    turn(1)
    differentiate(1)
    for copy in own_copies(1):
        copy.start()

    for f in range(12):
        stage_copy(f).wait()

        def move(t, _):
            p = pl.multiple_of(t * 64, 64)
            block = stage[f % 2, pl.ds(p, 64)].astype(jnp.float32)
            base[f, :, pl.ds(p, 64), :] = jnp.swapaxes(block, 0, 1).astype(jnp.bfloat16)
            return 0
        lax.fori_loop(0, 4, move, 0)
        if f + 2 < 12:
            stage_copy(f + 2).start()

    for g in range(4):
        own = four_rows(geometry_ref[g, pl.ds(pair(me), 8), :], me)
        for n in range(4):
            geo[g, n] = own[n : n + 1]

    relays(0)
    send_rows(1)
    send_slopes(1)
    lists_start(rim_ref, lists_state)
    rim_start()
    lists_part(count_block)
    compute(0, lambda g: None)
    relays(1)
    for g in range(2):
        send_back(0, g)
    lists_part(list_block)
    lists_end(rim_ref, lists_state, lists_ref)
    compute(1, lambda g: send_back(1, g))

    for h in range(HALVES):
        for g in range(2):
            own_back(h, g).wait()
            finish(h, g, me)

            def arrive(t, _):
                src = (me + t) % GROUP
                back_wait(h, g, src)
                finish(h, g, src)
                return 0
            lax.fori_loop(1, GROUP, arrive, 0)
    rim_total()

    for side in range(2):
        rim_copy(side).start()
    for side in range(2):
        rim_copy(side).wait_recv()
        rim_copy(side).wait_send()
    rims_ref[...] = rims[...] + met[...]

    for h in range(HALVES):
        for dx, k in SENT:
            row_copy(h, dx, k).wait_send()
        own_relay(h).wait_send()
        for dx, k in NEAR:
            relay(h, dx, k).wait_send()
        each(lambda t: slope_copy(h, t).wait_send())
        for g in range(2):
            each(lambda t: back_copy(h, g, t).wait_send())

            def drained(s, _):
                table_copy(h, g, s).wait()
                return 0
            lax.fori_loop(0, GROUP, drained, 0)


def step(u, base, geometry, mass, ids, rim):
    synth, anal = plane_tables()
    vmem = pl.BlockSpec(memory_space=pltpu.VMEM)
    hbm = pl.BlockSpec(memory_space=pl.ANY)
    f32 = jnp.float32
    dma = pltpu.SemaphoreType.DMA
    return pl.pallas_call(
        step_kernel,
        out_shape=(
            jax.ShapeDtypeStruct((POINTS, 128), f32),
            jax.ShapeDtypeStruct((2 * LIST_ROWS + 8, 128), jnp.int32),
            jax.ShapeDtypeStruct((2 * RIM_PAD, 128), f32),
        ),
        in_specs=[hbm, hbm] + [vmem] * 6,
        out_specs=(hbm, vmem, vmem),
        scratch_shapes=[
            pltpu.VMEM((HALVES, 3, COEFS, NODES, LANES), f32),
            pltpu.VMEM((HALVES, 3, NODES, COEFS, LANES), f32),
            pltpu.VMEM((HALVES, 3, NODES, COEFS, LANES), f32),
            pltpu.VMEM((HALVES, GROUP, 3, COEFS, 8, LANES), f32),
            pltpu.VMEM((HALVES, GROUP, 3, 4, COEFS, LANES), f32),
            pltpu.VMEM((12, 4, PLANES, E_DEV), jnp.bfloat16),
            pltpu.VMEM((2, PLANES, 4, E_DEV), jnp.bfloat16),
            pltpu.VMEM((4, PLANES, 9 * LANES), f32),
            pltpu.VMEM((PLANES, 12 * LANES), f32),
            pltpu.VMEM((PLANES, 3 * LANES), f32),
            pltpu.VMEM((HALVES, 2, GROUP, 2, 3, COEFS, LANES), f32),
            pltpu.VMEM((HALVES, 2, GROUP, 2, 3, COEFS, LANES), f32),
            pltpu.VMEM((POINTS, 128), f32),
            dma((HALVES, 8)), dma((HALVES, 8)), dma((HALVES, GROUP)), dma((HALVES, 2, GROUP)),
            dma((HALVES, GROUP)), dma((HALVES, GROUP)), dma((HALVES, 2, GROUP)),
            dma((HALVES, 4)), dma((2,)), dma((HALVES, 2, GROUP)),
            dma((HALVES,)),
            pltpu.VMEM((4, 4, 1, E_DEV), f32),
            pltpu.VMEM((2 * RIM_PAD, 128), f32),
            pltpu.VMEM((2 * RIM_PAD, 192), f32),
            pltpu.VMEM((2 * RIM_PAD, 128), f32),
            pltpu.VMEM((2 * RIM_PAD, 128), f32),
            dma((2,)), dma((2,)),
            pltpu.VMEM((128, 128), f32),
            pltpu.VMEM((256, 128), f32),
            pltpu.VMEM((NODES, E_DEV), f32),
            pltpu.VMEM((128, 128), f32),
            pltpu.VMEM((512, 128), f32),
            pltpu.VMEM((8, 128), f32),
        ],
        compiler_params=pltpu.CompilerParams(
            collective_id=0, has_side_effects=True, vmem_limit_bytes=VMEM_LIMIT
        ),
        name="step",
    )(u, base, geometry, mass, ids, rim, jnp.asarray(synth), jnp.asarray(anal))


def iota(shape, dim):
    return lax.broadcasted_iota(jnp.int32, shape, dim)


def flat(left, right):
    return lax.dot_general(left, right, (((1,), (1,)), ((), ())), preferred_element_type=jnp.float32)


def digits(ids):
    digit = iota((128, ids.shape[1]), 0)
    return (digit == ids // 128).astype(jnp.bfloat16), (digit == ids % 128).astype(jnp.bfloat16)


def look_up(tables, high, low):
    found = jnp.dot(tables.astype(jnp.bfloat16), high, preferred_element_type=jnp.float32)
    return [
        jnp.sum(found[k : k + 128] * low, axis=0, keepdims=True) for k in range(0, tables.shape[0], 128)
    ]


def place_of(n):
    lane = iota((1, E_DEV), 1)
    return ((lane // LANES) * NODES + n).astype(jnp.float32), (lane % LANES).astype(jnp.float32)


def count_block(i, ids_ref, state):
    counts, firsts, priors = state[0], state[1], state[2]
    at = pl.ds(pl.multiple_of(i * 8, 8), 8)
    tile = ids_ref[at, :]
    kept = []
    for j in range(8):
        ids = tile[j : j + 1]
        high, low = digits(ids)
        low_f = low.astype(jnp.float32)
        across = jnp.broadcast_to(ids.astype(jnp.float32), (E_DEV, E_DEV))
        earlier = iota((E_DEV, E_DEV), 0) < iota((E_DEV, E_DEV), 1)
        same = jnp.where((across == across.T) & earlier, 1.0, 0.0)
        prior = look_up(counts[...], high, low_f)[0] + jnp.sum(same, axis=0, keepdims=True)
        counts[...] = counts[...] + flat(low, high)
        block, inner = place_of(i * 8 + j)
        once = jnp.where(prior == 0, 1.0, 0.0)
        marks = jnp.concatenate([low_f * (once * block), low_f * (once * inner)])
        firsts[...] = firsts[...] + flat(marks.astype(jnp.bfloat16), high)
        kept.append(prior)
    priors[at, :] = jnp.concatenate(kept)


def list_block(i, ids_ref, state):
    counts, firsts, priors, on_rim, lists, used = state
    bf, f32 = jnp.bfloat16, jnp.float32
    at = pl.ds(pl.multiple_of(i * 8, 8), 8)
    tile, before_it = ids_ref[at, :], priors[at, :]
    for j in range(8):
        high, low = digits(tile[j : j + 1])
        low_f = low.astype(f32)
        prior = before_it[j : j + 1]
        tables = jnp.concatenate([counts[...], on_rim[...], firsts[...]])
        total, rim, rep_block, rep_inner = look_up(tables, high, low_f)
        again = jnp.where(prior > 0, 1.0, 0.0)
        lone = again * jnp.where((total == 2) & (rim == 0), 1.0, 0.0)
        kinds = jnp.concatenate([lone, again - lone, jnp.zeros((6, E_DEV), f32)])
        earlier = iota((E_DEV, E_DEV), 0) < iota((E_DEV, E_DEV), 1)
        before = jnp.dot(
            kinds.astype(bf), jnp.where(earlier, 1.0, 0.0).astype(bf), preferred_element_type=f32
        ) + used[:, 0:1]
        used[...] = used[...] + jnp.sum(kinds, axis=1, keepdims=True)
        slot = jnp.where(lone > 0, before[0:1], LISTED - 1 - before[1:2]).astype(jnp.int32)
        slot_high, slot_low = digits(slot)
        slot_low = slot_low.astype(f32) * again
        block, inner = place_of(i * 8 + j)
        left = jnp.concatenate([slot_low * v for v in (block, inner, rep_block, rep_inner)]).astype(bf)
        lists[...] = lists[...] + flat(left, slot_high)


def lists_start(rim_ref, state):
    for ref in state:
        ref[...] = jnp.zeros_like(ref)
    for k in range(2):
        high, low = digits(rim_ref[0][k : k + 1])
        state[3][...] = state[3][...] + flat(low, high)


def lists_end(rim_ref, state, lists_ref):
    counts, firsts, priors, on_rim, lists, used = state
    index = iota((128, 128), 0) * 128 + iota((128, 128), 1)
    front = used[0:1, 0:1].astype(jnp.int32)
    end = LISTED - used[1:2, 0:1].astype(jnp.int32)
    for k in range(2):
        at = lists[256 * k : 256 * k + 128] * 128.0 + lists[256 * k + 128 : 256 * k + 256]
        filled = (index < front) | (index >= end)
        entries = jnp.where(filled, at.T.astype(jnp.int32), POINTS)
        lists_ref[k * LIST_ROWS : (k + 1) * LIST_ROWS] = jnp.where(index < LISTED, entries, front)[0:LIST_ROWS]
    lists_ref[2 * LIST_ROWS :] = jnp.zeros((8, 128), jnp.int32)
    for k in range(2):
        high, low = digits(rim_ref[0][k : k + 1])
        rep_block, rep_inner = look_up(firsts[...], high, low.astype(jnp.float32))
        at = (rep_block * 128.0 + rep_inner).astype(jnp.int32)
        begin = 2 * LIST_ROWS + 2 * k
        lists_ref[begin : begin + 1] = at[:, 0:128]
        lists_ref[begin + 1 : begin + 2, 0 : RIM - 128] = at[:, 128:RIM]


def assemble_kernel(lists_ref, table_ref, rims_ref, out_ref, table, out, sem, out_sem):
    load = pltpu.make_async_copy(table_ref, table.at[pl.ds(0, POINTS)], sem.at[0])
    load.start()
    table[pl.ds(POINTS, 8)] = jnp.zeros((8, 1, 128), jnp.float32)
    load.wait()
    front = lists_ref[PLACES - 1]

    def entries(first):
        return [lists_ref[first + k] for k in range(BATCH)], [lists_ref[PLACES + first + k] for k in range(BATCH)]

    def pairs(t, _):
        places, reps = entries(t * BATCH)
        vals = [table[reps[k]] + table[places[k]] for k in range(BATCH)]
        for k in range(BATCH):
            table[reps[k]] = vals[k]
            table[places[k]] = vals[k]
        return 0
    lax.fori_loop(0, (front + BATCH - 1) // BATCH, pairs, 0)

    def add(t, _):
        at = lists_ref[PLACES + LISTED - 1 - t]
        table[at] = table[at] + table[lists_ref[LISTED - 1 - t]]
        return 0
    lax.fori_loop(0, EXTRA - front, add, 0)

    def meet(t, _):
        for side in range(2):
            for k in range(9):
                table[lists_ref[2 * PLACES + side * RIM_PAD + t * 9 + k]] = rims_ref[side * RIM_PAD + t * 9 + k]
        return 0
    lax.fori_loop(0, RIM // 9, meet, 0)

    def spread(t, _):
        places, reps = entries(LISTED - BATCH - t * BATCH)
        vals = [table[reps[k]] for k in range(BATCH)]
        for k in range(BATCH):
            table[places[k]] = vals[k]
        return 0
    lax.fori_loop(0, (EXTRA - front + BATCH - 1) // BATCH, spread, 0)

    def block_copy(t):
        at = (
            slice(None),
            pl.ds(pl.multiple_of((t % 8) * 8, 8), 8),
            pl.ds(pl.multiple_of((t // 8) * LANES, LANES), LANES),
        )
        return pltpu.make_async_copy(out.at[at], out_ref.at[at], out_sem.at[t])

    def write(t, _):
        h, i = t // 8, t % 8
        parts = []
        for j in range(8):
            begin = pl.multiple_of((h * NODES + i * 8 + j) * LANES, LANES)
            cols = table[pl.ds(begin, LANES)].reshape(LANES, 128).T
            parts.append(cols[0:48] / cols[48:49])
        block = jnp.swapaxes(jnp.stack(parts), 0, 1)
        out[:, pl.ds(pl.multiple_of(i * 8, 8), 8), pl.ds(pl.multiple_of(h * LANES, LANES), LANES)] = block
        block_copy(t).start()
        return 0
    lax.fori_loop(0, 16, write, 0)

    def written(t, _):
        block_copy(t).wait()
        return 0
    lax.fori_loop(0, 16, written, 0)


def assemble(table, lists, rims):
    smem = pl.BlockSpec(memory_space=pltpu.SMEM)
    vmem = pl.BlockSpec(memory_space=pltpu.VMEM)
    hbm = pl.BlockSpec(memory_space=pl.ANY)
    f32 = jnp.float32
    return pl.pallas_call(
        assemble_kernel,
        out_shape=jax.ShapeDtypeStruct((3 * COEFS, NODES, E_DEV), f32),
        in_specs=[smem, hbm, vmem],
        out_specs=hbm,
        scratch_shapes=[
            pltpu.VMEM((POINTS + 8, 1, 128), f32),
            pltpu.VMEM((3 * COEFS, NODES, E_DEV), f32),
            pltpu.SemaphoreType.DMA((1,)),
            pltpu.SemaphoreType.DMA((16,)),
        ],
        compiler_params=pltpu.CompilerParams(vmem_limit_bytes=VMEM_LIMIT),
        name="assemble",
    )(
        lists.reshape(-1), table.reshape(POINTS, 1, 128), rims.reshape(2 * RIM_PAD, 1, 128),
    )


def body(adj_modes, base_flow, geometry, mass, connect, edge_nodes):
    table, lists, rims = step(adj_modes, base_flow, geometry, mass, connect, edge_nodes)
    return assemble(table, lists, rims).reshape(adj_modes.shape)


def solution(mesh):
    return jax.shard_map(
        body,
        mesh=mesh,
        in_specs=(
            P(None, "four", None, "mesh"),
            P(None, None, "four", "mesh"),
            P(None, None, "mesh"),
            P(None, "mesh"),
            P(None, "mesh"),
            P("mesh", None, None),
        ),
        out_specs=P(None, "four", None, "mesh"),
        check_vma=False,
    )
```

time: 295 us -> 289 us (0.980)
  Pallas kernels: 293 us -> 288 us
    pallas_call x1, Pallas kernels: 265 us -> 261 us  [step(): pl.pallas_call(step_kernel, out_shape=(jax.ShapeDtypeStruct((POINTS, 128)...]
where the time goes in v3:
time: 289 us; the launch traced here: 288 us
  Pallas kernels  288 us (100%)
    pallas_call x1, Pallas kernels, step(): pl.pallas_call(step_kernel, out_shape=(jax.ShapeDtypeStruct((POINTS, 128)...  261 us
    pallas_call x1, Pallas kernels, assemble(): pl.pallas_call(assemble_kernel, out_shape=jax.ShapeDtypeStruct((3 * COEFS...  26.8 us

profile of v3, /device:TPU:2, one launch (start us, length us, event | category | flops | bytes accessed | tf_op | source)
XLA Modules:
  0.0 288.4 jit_solution(16574786100221870552)
XLA Ops:
  0.0 261.4 %step.1 = (f32[16384,128]{1,0:T(8,128)}, s32[72,128]{1,0:T(8,128)}, f32[512,128]{1,0:T(8,128)}) custom-call(f32[3,16,64,256]{3,2,1,0:T(8,128)} %u_ref.1, bf16[12,256,4,256]{3,2,1,0:T(4,128)(2,1)} %base_ref.1, f32[4,64,256]{2,1,0:T(8,128)} %geometry_ref.1, f32[64,256]{1,0:T(8,128)} %mass_ref.1, s32[64,256]{1,0:T(8,128)} %ids_ref.1, s32[1,2,225]{2,1,0:T(2,128)} %rim_ref.1, ...), custom_call_target="tpu_custom_call" | custom-call | tf_op jit(solution)/shard_map/step/pallas_call | solution.py:427
  261.4 26.8 %assemble.1 = f32[48,64,256]{2,1,0:T(8,128)} custom-call(s32[9216]{0:T(1024)} %bitcast.6, f32[16384,1,128]{2,1,0:T(1,128)} %bitcast.4, f32[512,1,128]{2,1,0:T(1,128)} %bitcast.5), custom_call_target="tpu_custom_call" | custom-call | tf_op jit(solution)/shard_map/assemble/pallas_call | solution.py:648

commit v4 on v3

--- a/solution.py
+++ b/solution.py
@@ -383,6 +383,25 @@
     compute(1, lambda g: send_back(1, g))
 
     for h in range(HALVES):
+        for dx, k in SENT:
+            row_copy(h, dx, k).wait_send()
+        own_relay(h).wait_send()
+        for dx, k in NEAR:
+            relay(h, dx, k).wait_send()
+        each(lambda t: slope_copy(h, t).wait_send())
+
+    def returns_sent(h):
+        for g in range(2):
+            each(lambda t: back_copy(h, g, t).wait_send())
+
+            def drained(s, _):
+                table_copy(h, g, s).wait()
+                return 0
+            lax.fori_loop(0, GROUP, drained, 0)
+
+    for h in range(HALVES):
+        if h == 1:
+            returns_sent(0)
         for g in range(2):
             own_back(h, g).wait()
             finish(h, g, me)
@@ -397,25 +416,11 @@
 
     for side in range(2):
         rim_copy(side).start()
+    returns_sent(1)
     for side in range(2):
         rim_copy(side).wait_recv()
         rim_copy(side).wait_send()
     rims_ref[...] = rims[...] + met[...]
-
-    for h in range(HALVES):
-        for dx, k in SENT:
-            row_copy(h, dx, k).wait_send()
-        own_relay(h).wait_send()
-        for dx, k in NEAR:
-            relay(h, dx, k).wait_send()
-        each(lambda t: slope_copy(h, t).wait_send())
-        for g in range(2):
-            each(lambda t: back_copy(h, g, t).wait_send())
-
-            def drained(s, _):
-                table_copy(h, g, s).wait()
-                return 0
-            lax.fori_loop(0, GROUP, drained, 0)
 
 
 def step(u, base, geometry, mass, ids, rim):
@@ -593,10 +598,12 @@
     lax.fori_loop(0, (front + BATCH - 1) // BATCH, pairs, 0)
 
     def add(t, _):
-        at = lists_ref[PLACES + LISTED - 1 - t]
-        table[at] = table[at] + table[lists_ref[LISTED - 1 - t]]
+        places, reps = entries(LISTED - BATCH - t * BATCH)
+        vals = [table[places[k]] for k in range(BATCH)]
+        for k in range(BATCH):
+            table[reps[k]] = table[reps[k]] + vals[k]
         return 0
-    lax.fori_loop(0, EXTRA - front, add, 0)
+    lax.fori_loop(0, (EXTRA - front + BATCH - 1) // BATCH, add, 0)
 
     def meet(t, _):
         for side in range(2):

time: 289 us -> 286 us (0.990)
  Pallas kernels: 288 us -> 285 us
where the time goes in v4:
time: 286 us; the launch traced here: 285 us
  Pallas kernels  285 us (100%)
    pallas_call x1, Pallas kernels, step(): pl.pallas_call(step_kernel, out_shape=(jax.ShapeDtypeStruct((POINTS, 128)...  260 us
    pallas_call x1, Pallas kernels, assemble(): pl.pallas_call(assemble_kernel, out_shape=jax.ShapeDtypeStruct((3 * COEFS...  24.4 us

profile of v4, /device:TPU:2, one launch (start us, length us, event | category | flops | bytes accessed | tf_op | source)
XLA Modules:
  0.0 284.9 jit_solution(5847833440535845551)
XLA Ops:
  0.0 260.3 %step.1 = (f32[16384,128]{1,0:T(8,128)}, s32[72,128]{1,0:T(8,128)}, f32[512,128]{1,0:T(8,128)}) custom-call(f32[3,16,64,256]{3,2,1,0:T(8,128)} %u_ref.1, bf16[12,256,4,256]{3,2,1,0:T(4,128)(2,1)} %base_ref.1, f32[4,64,256]{2,1,0:T(8,128)} %geometry_ref.1, f32[64,256]{1,0:T(8,128)} %mass_ref.1, s32[64,256]{1,0:T(8,128)} %ids_ref.1, s32[1,2,225]{2,1,0:T(2,128)} %rim_ref.1, ...), custom_call_target="tpu_custom_call" | custom-call | tf_op jit(solution)/shard_map/step/pallas_call | solution.py:432
  260.3 24.4 %assemble.1 = f32[48,64,256]{2,1,0:T(8,128)} custom-call(s32[9216]{0:T(1024)} %bitcast.6, f32[16384,1,128]{2,1,0:T(1,128)} %bitcast.4, f32[512,1,128]{2,1,0:T(1,128)} %bitcast.5), custom_call_target="tpu_custom_call" | custom-call | tf_op jit(solution)/shard_map/assemble/pallas_call | solution.py:655
